TPU v7x, 128 devices: a whole 4x4x4 slice. The times are simulated.
128 devices in a mesh: dp: 4 (over z), expert: 32 (over y, x, core).
Axes of the slice: x: 4, y: 4, z: 4, core: 2. Of those that a mesh axis runs over, the one named last changes fastest.
Arguments:
- tokens: bfloat16 [3072, 4096], P(('dp', 'expert')), may hold values from -6 to 6
- out_grad: bfloat16 [3072, 4096], P(('dp', 'expert')), may hold values from -1.5 to 1.5
- routes: int32 [3072, 8], P(('dp', 'expert')), may hold values from 0 to 63, all different within a row; in each aligned block of 24 rows (0 to 23, 24 to 47, ...) at most 6 rows name the same one
- gate_probs: bfloat16 [3072, 8], P(('dp', 'expert')), may hold values from 0.049804688 to 0.29882812
- gate_weight: bfloat16 [128, 4096, 384], P(('dp', 'expert')), may hold values from -0.09375 to 0.09375
- up_weight: bfloat16 [128, 4096, 384], P(('dp', 'expert')), may hold values from -0.09375 to 0.09375
- down_weight: bfloat16 [128, 384, 4096], P(('dp', 'expert')), may hold values from -0.21875 to 0.21875
Outputs:
- token_grad: bfloat16 [3072, 4096], P(('dp', 'expert'))
- prob_grad: float32 [3072, 8], P(('dp', 'expert'))
- gate_grad: bfloat16 [128, 4096, 384], P(('dp', 'expert'))
- up_grad: bfloat16 [128, 4096, 384], P(('dp', 'expert'))
- down_grad: bfloat16 [128, 384, 4096], P(('dp', 'expert'))
Inputs may be any that keep to these rules, and one draw needn't show every extreme that they name: `routes`: each token names 8 different experts; in the rows of one device no expert is named by more than 6 slots, a bound that some block reaches of them.
All inputs are finite; a program needn't handle non-finite values.
Results may differ from a plain program's by a relative error of at most 0.0057.
Values may be sent and summed in bfloat16 or wider, within the bound.
A program may use at most 192 MiB of HBM per device.

v0:
```python
import jax
import jax.numpy as jnp
from jax import lax
from jax.sharding import PartitionSpec as P


def half_terms(rows_in, grads_in, probs_in, gate_half, up_half, down_half):
    gate_pre = jnp.dot(rows_in, gate_half, preferred_element_type=jnp.float32)
    up_pre = jnp.dot(rows_in, up_half, preferred_element_type=jnp.float32)
    sigmoid = jax.nn.sigmoid(gate_pre)
    active = gate_pre * sigmoid
    hidden = active * up_pre
    raw_grad = lax.dot_general(
        grads_in, down_half, (((1,), (1,)), ((), ())), preferred_element_type=jnp.float32
    )
    prob_part = jnp.sum(hidden * raw_grad, axis=1).astype(jnp.bfloat16)
    weight = probs_in.astype(jnp.float32)[:, None]
    scaled_grad = weight * raw_grad
    gate_delta = (scaled_grad * up_pre * sigmoid * (1.0 + gate_pre * (1.0 - sigmoid))).astype(
        jnp.bfloat16
    )
    up_delta = (scaled_grad * active).astype(jnp.bfloat16)
    scaled_hidden = (weight * hidden).astype(jnp.bfloat16)
    gate_sum = lax.dot_general(
        rows_in, gate_delta, (((0,), (0,)), ((), ())), preferred_element_type=jnp.float32
    )
    up_sum = lax.dot_general(
        rows_in, up_delta, (((0,), (0,)), ((), ())), preferred_element_type=jnp.float32
    )
    down_sum = lax.dot_general(
        scaled_hidden, grads_in, (((0,), (0,)), ((), ())), preferred_element_type=jnp.float32
    )
    input_part = (
        lax.dot_general(
            gate_delta, gate_half, (((1,), (1,)), ((), ())), preferred_element_type=jnp.float32
        )
        + lax.dot_general(
            up_delta, up_half, (((1,), (1,)), ((), ())), preferred_element_type=jnp.float32
        )
    ).astype(jnp.bfloat16)
    return (gate_sum, up_sum, down_sum, input_part, prob_part)


def pair_copies(values, expert_count, capacity):
    shaped = values.reshape((expert_count, 1, capacity) + values.shape[1:])
    doubled = jnp.broadcast_to(shaped, (expert_count, 2, capacity) + values.shape[1:])
    return doubled.reshape((2 * expert_count, capacity) + values.shape[1:])


def on_device(tokens, out_grad, routes, gate_probs, gate_weight, up_weight, down_weight):
    tok_count, model_width = tokens.shape
    top_count = routes.shape[1]
    device_count = lax.axis_size("dp") * lax.axis_size("expert")
    expert_count = device_count // 2
    capacity = 2 * tok_count * top_count // expert_count
    slot_count = tok_count * top_count
    buffer_len = expert_count * capacity
    chosen = routes.reshape(slot_count)
    onehot = (chosen[:, None] == jnp.arange(expert_count, dtype=jnp.int32)[None, :]).astype(
        jnp.int32
    )
    slot_rank = jnp.sum((jnp.cumsum(onehot, axis=0) - onehot) * onehot, axis=1)
    target = chosen * capacity + slot_rank
    placing = (jnp.arange(buffer_len, dtype=jnp.int32)[:, None] == target[None, :]).astype(
        jnp.bfloat16
    )
    token_place = jnp.sum(placing.reshape(buffer_len, tok_count, top_count), axis=2)
    sent_rows = jnp.dot(token_place, tokens, preferred_element_type=jnp.float32).astype(
        jnp.bfloat16
    )
    sent_grads = jnp.dot(token_place, out_grad, preferred_element_type=jnp.float32).astype(
        jnp.bfloat16
    )
    sent_probs = jnp.dot(
        placing, gate_probs.reshape(slot_count), preferred_element_type=jnp.float32
    ).astype(jnp.bfloat16)
    got_rows, got_grads, got_probs = (
        lax.all_to_all(
            pair_copies(sent_rows, expert_count, capacity),
            ("dp", "expert"),
            split_axis=0,
            concat_axis=0,
            tiled=True,
        ),
        lax.all_to_all(
            pair_copies(sent_grads, expert_count, capacity),
            ("dp", "expert"),
            split_axis=0,
            concat_axis=0,
            tiled=True,
        ),
        lax.all_to_all(
            pair_copies(sent_probs, expert_count, capacity),
            ("dp", "expert"),
            split_axis=0,
            concat_axis=0,
            tiled=True,
        ),
    )
    rows_in = got_rows.reshape(-1, model_width)
    grads_in = got_grads.reshape(-1, model_width)
    probs_in = got_probs.reshape(-1)
    gate_half = gate_weight[0]
    up_half = up_weight[0]
    down_half = down_weight[0]
    gate_sum, up_sum, down_sum, input_part, prob_part = half_terms(
        rows_in, grads_in, probs_in, gate_half, up_half, down_half
    )
    back_input, back_prob = (
        lax.all_to_all(
            input_part.reshape(device_count, capacity, model_width),
            ("dp", "expert"),
            split_axis=0,
            concat_axis=0,
            tiled=True,
        ),
        lax.all_to_all(
            prob_part.reshape(device_count, capacity),
            ("dp", "expert"),
            split_axis=0,
            concat_axis=0,
            tiled=True,
        ),
    )
    slot_input = jnp.sum(
        back_input.reshape(expert_count, 2, capacity, model_width).astype(jnp.float32), axis=1
    ).reshape(buffer_len, model_width)
    slot_prob = jnp.sum(
        back_prob.reshape(expert_count, 2, capacity).astype(jnp.float32), axis=1
    ).reshape(buffer_len)
    token_grad = jnp.dot(
        token_place.astype(jnp.float32).T, slot_input, precision=lax.Precision.HIGHEST
    ).astype(jnp.bfloat16)
    prob_grad = jnp.dot(
        placing.astype(jnp.float32).T, slot_prob, precision=lax.Precision.HIGHEST
    ).reshape(tok_count, top_count)
    return (
        token_grad,
        prob_grad,
        gate_sum.astype(jnp.bfloat16)[None],
        up_sum.astype(jnp.bfloat16)[None],
        down_sum.astype(jnp.bfloat16)[None],
    )


def solution(mesh):
    return jax.shard_map(
        on_device,
        mesh=mesh,
        in_specs=(
            P(("dp", "expert"), None),
            P(("dp", "expert"), None),
            P(("dp", "expert"), None),
            P(("dp", "expert"), None),
            P(("dp", "expert"), None, None),
            P(("dp", "expert"), None, None),
            P(("dp", "expert"), None, None),
        ),
        out_specs=(
            P(("dp", "expert"), None),
            P(("dp", "expert"), None),
            P(("dp", "expert"), None, None),
            P(("dp", "expert"), None, None),
            P(("dp", "expert"), None, None),
        ),
        check_vma=False,
    )
```

profile of v0, /device:TPU:0, one launch (start us, length us, event | category | flops | bytes accessed | tf_op | source)
XLA Modules:
  0.0 449.6 jit_solution(6507844830658129954)
XLA Ops:
  0.6 0.9 copy.36
  1.7 0.8 copy.32
  4.6 11.1 %all-to-all-start = ((bf16[128,1,6]{2,1,0:T(2,128)(2,1)}), bf16[128,1,6]{2,1,0:T(2,128)(2,1)S(1)}, u32[]{:S(2)}, u32[]{:S(2)}) async-start(bf16[128,1,6]{2,1,0:T(2,128)(2,1)} %copy.37), calls=%async_computation | async-start | bytes 131072 | tf_op jit(solution)/shard_map/all_to_all | solution.py:92
  16.0 3.6 convolution_convert_fusion
  19.6 5.6 %broadcast_in_dim.38 = bf16[64,6,4096]{2,1,0:T(8,128)(2,1)} reshape(bf16[384,4096]{1,0:T(8,128)(2,1)} %convolution_convert_fusion) | data formatting | bytes 6291456 | tf_op jit(solution)/shard_map/broadcast_in_dim | solution.py:46
  25.3 6.5 %broadcast_in_dim.39 = bf16[64,2,6,4096]{3,2,1,0:T(8,128)(2,1)} broadcast(bf16[64,6,4096]{2,1,0:T(8,128)(2,1)} %broadcast_in_dim.38), dimensions={0,2,3} | broadcast | bytes 9437184 | tf_op jit(solution)/shard_map/broadcast_in_dim | solution.py:46
  31.7 10.3 %all-to-all-start.2 = ((bf16[128,6,4096]{2,1,0:T(8,128)(2,1)}), bf16[128,6,4096]{2,1,0:T(8,128)(2,1)}, u32[]{:S(2)}, u32[]{:S(2)}) async-start(bf16[128,6,4096]{2,1,0:T(8,128)(2,1)} %bitcast.63), calls=%async_computation.2 | async-start | bytes 16777216 | tf_op jit(solution)/shard_map/all_to_all | solution.py:78
  42.1 2.7 convolution_convert_fusion.1
  44.7 5.7 %broadcast_in_dim.36 = bf16[64,6,4096]{2,1,0:T(8,128)(2,1)} reshape(bf16[384,4096]{1,0:T(8,128)(2,1)} %convolution_convert_fusion.1) | data formatting | bytes 6291456 | tf_op jit(solution)/shard_map/broadcast_in_dim | solution.py:46
  50.4 90.1 %all-to-all-done.2 = bf16[128,6,4096]{2,1,0:T(8,128)(2,1)} async-done(((bf16[128,6,4096]{2,1,0:T(8,128)(2,1)}), bf16[128,6,4096]{2,1,0:T(8,128)(2,1)}, u32[]{:S(2)}, u32[]{:S(2)}) %all-to-all-start.2) | async-done | bytes 6291488 | tf_op jit(solution)/shard_map/all_to_all | solution.py:78
  140.5 6.5 %broadcast_in_dim.37 = bf16[64,2,6,4096]{3,2,1,0:T(8,128)(2,1)} broadcast(bf16[64,6,4096]{2,1,0:T(8,128)(2,1)} %broadcast_in_dim.36), dimensions={0,2,3} | broadcast | bytes 9437184 | tf_op jit(solution)/shard_map/broadcast_in_dim | solution.py:46
  146.9 14.0 %all-to-all-start.1 = ((bf16[128,6,4096]{2,1,0:T(8,128)(2,1)}), bf16[128,6,4096]{2,1,0:T(8,128)(2,1)}, u32[]{:S(2)}, u32[]{:S(2)}) async-start(bf16[128,6,4096]{2,1,0:T(8,128)(2,1)} %bitcast.62), calls=%async_computation.1 | async-start | bytes 16777216 | tf_op jit(solution)/shard_map/all_to_all | solution.py:85
  161.3 10.2 %reshape.136 = bf16[768,4096]{1,0:T(8,128)(2,1)} reshape(bf16[128,6,4096]{2,1,0:T(8,128)(2,1)} %all-to-all-done.2) | data formatting | bytes 12582912 | tf_op jit(solution)/shard_map/reshape | solution.py:100
  171.5 6.6 %fusion.5 = f32[768,384]{0,1:T(8,128)} fusion(bf16[768,4096]{1,0:T(8,128)(2,1)} %reshape.136, bf16[1,4096,384]{2,1,0:T(8,128)(2,1)S(1)} %copy-done), kind=kOutput, calls=%fused_computation.13 | convolution fusion | flops 2415919104 | bytes 10616832 | tf_op jit(solution)/shard_map/dot_general | solution.py:8
  178.1 3.6 fusion.8
  181.8 77.5 %all-to-all-done.1 = bf16[128,6,4096]{2,1,0:T(8,128)(2,1)} async-done(((bf16[128,6,4096]{2,1,0:T(8,128)(2,1)}), bf16[128,6,4096]{2,1,0:T(8,128)(2,1)}, u32[]{:S(2)}, u32[]{:S(2)}) %all-to-all-start.1) | async-done | bytes 6291488 | tf_op jit(solution)/shard_map/all_to_all | solution.py:85
  259.3 10.3 %reshape.134 = bf16[768,4096]{1,0:T(8,128)(2,1)} reshape(bf16[128,6,4096]{2,1,0:T(8,128)(2,1)} %all-to-all-done.1) | data formatting | bytes 12582912 | tf_op jit(solution)/shard_map/reshape | solution.py:101
  269.5 8.4 %multiply_reduce_fusion = (bf16[768]{0:T(1024)(128)(2,1)S(1)}, bf16[768,384]{0,1:T(8,128)(2,1)}, bf16[768,384]{0,1:T(8,128)(2,1)}) fusion(f32[768,384]{0,1:T(8,128)} %fusion.8, f32[768,384]{0,1:T(8,128)} %fusion.5, f32[768]{0:T(1024)S(1)} %reshape.141, bf16[768,4096]{1,0:T(8,128)(2,1)} %reshape.134, bf16[1,384,4096]{2,1,0:T(8,128)(2,1)} %param.13), kind=kOutput, calls=%fused_computation.21 | convolution fusion | flops 2420931840 | bytes 12980736 | tf_op jit(solution)/shard_map/dot_general | solution.py:13
  277.9 0.8 convert_element_type.108
  278.7 13.1 %all-to-all-start.4 = ((bf16[128,1,6]{2,1,0:T(2,128)(2,1)}), bf16[128,1,6]{2,1,0:T(2,128)(2,1)S(1)}, u32[]{:S(2)}, u32[]{:S(2)}) async-start(bf16[128,1,6]{2,1,0:T(2,128)(2,1)} %convert_element_type.108), calls=%async_computation.4 | async-start | bytes 131072 | tf_op jit(solution)/shard_map/all_to_all | solution.py:117
  291.9 7.6 %fusion.3 = f32[768,4096]{1,0:T(8,128)} fusion(bf16[768,384]{0,1:T(8,128)(2,1)} %get-tuple-element.6, bf16[1,4096,384]{2,1,0:T(8,128)(2,1)S(1)} %copy-done), kind=kOutput, calls=%fused_computation.11 | convolution fusion | flops 2415919104 | bytes 16318464 | tf_op jit(solution)/shard_map/dot_general | solution.py:34
  299.5 8.2 %add_convert_fusion = bf16[768,4096]{1,0:T(8,128)(2,1)} fusion(f32[768,4096]{1,0:T(8,128)} %fusion.3, bf16[768,384]{0,1:T(8,128)(2,1)S(1)} %copy-done.5, bf16[1,4096,384]{2,1,0:T(8,128)(2,1)S(1)} %copy-done.4), kind=kOutput, calls=%fused_computation.1 | convolution fusion | flops 2422210560 | bytes 22609920 | tf_op jit(solution)/shard_map/dot_general | solution.py:37
  307.8 10.1 %reshape.137 = bf16[128,6,4096]{2,1,0:T(8,128)(2,1)} reshape(bf16[768,4096]{1,0:T(8,128)(2,1)} %add_convert_fusion) | data formatting | bytes 12582912 | tf_op jit(solution)/shard_map/reshape | solution.py:111
  317.9 10.1 %all-to-all-start.3 = ((bf16[128,6,4096]{2,1,0:T(8,128)(2,1)}), bf16[128,6,4096]{2,1,0:T(8,128)(2,1)}, u32[]{:S(2)}, u32[]{:S(2)}) async-start(bf16[128,6,4096]{2,1,0:T(8,128)(2,1)} %reshape.137), calls=%async_computation.3 | async-start | bytes 16777216 | tf_op jit(solution)/shard_map/all_to_all | solution.py:110
  328.0 8.1 %fusion = bf16[1,4096,384]{2,1,0:T(8,128)(2,1)} fusion(bf16[768,4096]{1,0:T(8,128)(2,1)} %reshape.136, bf16[768,384]{0,1:T(8,128)(2,1)S(1)} %copy-done.7), kind=kOutput, calls=%fused_computation.7 | convolution fusion | flops 2417491968 | bytes 10027008 | tf_op jit(solution)/shard_map/dot_general | solution.py:24
  336.1 8.1 %fusion.1 = bf16[1,4096,384]{2,1,0:T(8,128)(2,1)} fusion(bf16[768,4096]{1,0:T(8,128)(2,1)} %reshape.136, bf16[768,384]{0,1:T(8,128)(2,1)S(1)} %copy-done.6), kind=kOutput, calls=%fused_computation.8 | convolution fusion | flops 2417491968 | bytes 10027008 | tf_op jit(solution)/shard_map/dot_general | solution.py:27
  344.2 4.2 fusion.2
  348.7 1.5 fusion.17
  350.8 75.5 %all-to-all-done.3 = bf16[128,6,4096]{2,1,0:T(8,128)(2,1)} async-done(((bf16[128,6,4096]{2,1,0:T(8,128)(2,1)}), bf16[128,6,4096]{2,1,0:T(8,128)(2,1)}, u32[]{:S(2)}, u32[]{:S(2)}) %all-to-all-start.3) | async-done | bytes 6291488 | tf_op jit(solution)/shard_map/all_to_all | solution.py:110
  426.4 9.6 %convert_reduce_fusion = f32[64,6,4096]{2,1,0:T(8,128)} fusion(bf16[128,6,4096]{2,1,0:T(8,128)(2,1)} %all-to-all-done.3), kind=kLoop, calls=%fused_computation | loop fusion | flops 4718592 | bytes 12582912 | tf_op jit(solution)/shard_map/reduce_sum | solution.py:125
  435.9 8.1 %reshape.138 = f32[384,4096]{1,0:T(8,128)} reshape(f32[64,6,4096]{2,1,0:T(8,128)} %convert_reduce_fusion) | data formatting | bytes 12582912 | tf_op jit(solution)/shard_map/reshape | solution.py:127
  444.0 5.6 %convolution_convert_fusion.5 = bf16[24,4096]{1,0:T(8,128)(2,1)} fusion(bf16[384,24]{0,1:T(8,128)(2,1)S(1)} %fusion.20, f32[384,4096]{1,0:T(8,128)} %reshape.138), kind=kOutput, calls=%fused_computation.10 | convolution fusion | flops 453083136 | bytes 6506496 | tf_op jit(solution)/shard_map/dot_general | solution.py:131
  (53 shorter events, 3.8 us)
Async XLA Ops:
  0.6 170.9 %copy-start = (bf16[1,4096,384]{2,1,0:T(8,128)(2,1)S(1)}, bf16[1,4096,384]{2,1,0:T(8,128)(2,1)}, u32[]{:S(2)}) copy-start(bf16[1,4096,384]{2,1,0:T(8,128)(2,1)} %param.11) | copy-start | bytes 9437188
  4.6 20.7 %all-to-all-start = ((bf16[128,1,6]{2,1,0:T(2,128)(2,1)}), bf16[128,1,6]{2,1,0:T(2,128)(2,1)S(1)}, u32[]{:S(2)}, u32[]{:S(2)}) async-start(bf16[128,1,6]{2,1,0:T(2,128)(2,1)} %copy.37), calls=%async_computation | async-start | bytes 131072 | tf_op jit(solution)/shard_map/all_to_all | solution.py:92
  31.7 10.3 %copy-start.8 = (bf16[24,4096]{1,0:T(8,128)(2,1)S(1)}, bf16[24,4096]{1,0:T(8,128)(2,1)}, u32[]{:S(2)}) copy-start(bf16[24,4096]{1,0:T(8,128)(2,1)} %param.8) | copy-start | bytes 589828
  31.7 108.7 %all-to-all-start.2 = ((bf16[128,6,4096]{2,1,0:T(8,128)(2,1)}), bf16[128,6,4096]{2,1,0:T(8,128)(2,1)}, u32[]{:S(2)}, u32[]{:S(2)}) async-start(bf16[128,6,4096]{2,1,0:T(8,128)(2,1)} %bitcast.63), calls=%async_computation.2 | async-start | bytes 16777216 | tf_op jit(solution)/shard_map/all_to_all | solution.py:78
  146.9 112.3 %all-to-all-start.1 = ((bf16[128,6,4096]{2,1,0:T(8,128)(2,1)}), bf16[128,6,4096]{2,1,0:T(8,128)(2,1)}, u32[]{:S(2)}, u32[]{:S(2)}) async-start(bf16[128,6,4096]{2,1,0:T(8,128)(2,1)} %bitcast.62), calls=%async_computation.1 | async-start | bytes 16777216 | tf_op jit(solution)/shard_map/all_to_all | solution.py:85
  171.5 6.6 %copy-start.2 = (bf16[768,4096]{1,0:T(8,128)(2,1)S(1)}, bf16[768,4096]{1,0:T(8,128)(2,1)}, u32[]{:S(2)}) copy-start(bf16[768,4096]{1,0:T(8,128)(2,1)} %reshape.136) | copy-start | bytes 18874372
  171.5 6.6 %copy-start.3 = (bf16[1,4096,384]{2,1,0:T(8,128)(2,1)S(1)}, bf16[1,4096,384]{2,1,0:T(8,128)(2,1)}, u32[]{:S(2)}) copy-start(bf16[1,4096,384]{2,1,0:T(8,128)(2,1)} %param.12) | copy-start | bytes 9437188
  278.7 39.1 %all-to-all-start.4 = ((bf16[128,1,6]{2,1,0:T(2,128)(2,1)}), bf16[128,1,6]{2,1,0:T(2,128)(2,1)S(1)}, u32[]{:S(2)}, u32[]{:S(2)}) async-start(bf16[128,1,6]{2,1,0:T(2,128)(2,1)} %convert_element_type.108), calls=%async_computation.4 | async-start | bytes 131072 | tf_op jit(solution)/shard_map/all_to_all | solution.py:117
  291.9 7.6 %copy-start.4 = (bf16[1,4096,384]{2,1,0:T(8,128)(2,1)S(1)}, bf16[1,4096,384]{2,1,0:T(8,128)(2,1)}, u32[]{:S(2)}) copy-start(bf16[1,4096,384]{2,1,0:T(8,128)(2,1)} %param.12) | copy-start | bytes 9437188
  291.9 7.6 %copy-start.5 = (bf16[768,384]{0,1:T(8,128)(2,1)S(1)}, bf16[768,384]{0,1:T(8,128)(2,1)}, u32[]{:S(2)}) copy-start(bf16[768,384]{0,1:T(8,128)(2,1)} %get-tuple-element.7) | copy-start | bytes 1769476
  317.9 10.1 %copy-start.7 = (bf16[768,384]{0,1:T(8,128)(2,1)S(1)}, bf16[768,384]{0,1:T(8,128)(2,1)}, u32[]{:S(2)}) copy-start(bf16[768,384]{0,1:T(8,128)(2,1)} %get-tuple-element.6) | copy-start | bytes 1769476
  317.9 108.5 %all-to-all-start.3 = ((bf16[128,6,4096]{2,1,0:T(8,128)(2,1)}), bf16[128,6,4096]{2,1,0:T(8,128)(2,1)}, u32[]{:S(2)}, u32[]{:S(2)}) async-start(bf16[128,6,4096]{2,1,0:T(8,128)(2,1)} %reshape.137), calls=%async_computation.3 | async-start | bytes 16777216 | tf_op jit(solution)/shard_map/all_to_all | solution.py:110
  328.0 8.1 %copy-start.6 = (bf16[768,384]{0,1:T(8,128)(2,1)S(1)}, bf16[768,384]{0,1:T(8,128)(2,1)}, u32[]{:S(2)}) copy-start(bf16[768,384]{0,1:T(8,128)(2,1)} %get-tuple-element.7) | copy-start | bytes 1769476
  328.0 16.2 %slice-start = ((s8[6291456]{0:T(1024)(128)(4,1)}), s8[4194304]{0:T(1024)(128)(4,1)S(1)}, s32[]{:S(2)}) async-start(s8[6291456]{0:T(1024)(128)(4,1)} %bitcast.64), calls=%async_computation.5 | async-start | bytes 8388608
  336.1 8.1 %slice-start.1 = ((s8[6291456]{0:T(1024)(128)(4,1)}), s8[2097152]{0:T(1024)(128)(4,1)S(1)}, s32[]{:S(2)}) async-start(s8[6291456]{0:T(1024)(128)(4,1)} %bitcast.64), calls=%async_computation.6 | async-start | bytes 4194304
  336.1 8.1 %copy-start.9 = (f32[768,384]{0,1:T(8,128)S(1)}, f32[768,384]{0,1:T(8,128)}, u32[]{:S(2)}) copy-start(f32[768,384]{0,1:T(8,128)} %fusion.5) | copy-start | bytes 3538948
  336.1 8.1 %copy-start.10 = (f32[768,384]{0,1:T(8,128)S(1)}, f32[768,384]{0,1:T(8,128)}, u32[]{:S(2)}) copy-start(f32[768,384]{0,1:T(8,128)} %fusion.8) | copy-start | bytes 3538948
  435.9 13.7 %copy-start.1 = (bf16[1,4096,384]{2,1,0:T(8,128)(2,1)S(1)}, bf16[1,4096,384]{2,1,0:T(8,128)(2,1)}, u32[]{:S(2)}) copy-start(bf16[1,4096,384]{2,1,0:T(8,128)(2,1)} %param.11) | copy-start | bytes 9437188
where the time goes:
time: 455 us; the launch traced here: 450 us
  waiting for transfers between devices  243 us (53%)
  matrix products  68.4 us (15%)
  local copies, waits for them, and re-layouts  67.7 us (15%)
  starting transfers between devices  58.7 us (13%)
  other arithmetic  10.9 us (2%)
    all_to_all x1, waiting for transfers between devices, on_device(): lax.all_to_all(pair_copies(sent_rows, expert_count, capacity), ('dp', 'ex...  90.1 us
    all_to_all x1, waiting for transfers between devices, on_device(): lax.all_to_all(pair_copies(sent_grads, expert_count, capacity), ('dp', 'e...  77.5 us
    all_to_all x1, waiting for transfers between devices, on_device(): lax.all_to_all(input_part.reshape(device_count, capacity, model_width), (...  75.5 us
    broadcast_in_dim x6, local copies, waits for them, and re-layouts, pair_copies(): jnp.broadcast_to(shaped, (expert_count, 2, capacity) + values.shape[1:])  24.4 us
    all_to_all x1, starting transfers between devices, on_device(): lax.all_to_all(pair_copies(sent_grads, expert_count, capacity), ('dp', 'e...  14 us
    all_to_all x1, starting transfers between devices, on_device(): lax.all_to_all(prob_part.reshape(device_count, capacity), ('dp', 'expert'...  13.1 us
    all_to_all x1, starting transfers between devices, on_device(): lax.all_to_all(pair_copies(sent_probs, expert_count, capacity), ('dp', 'e...  11.1 us
    all_to_all x1, starting transfers between devices, on_device(): lax.all_to_all(pair_copies(sent_rows, expert_count, capacity), ('dp', 'ex...  10.3 us
  transfers between devices with their start and end apart: 5, of which 3 were waited for; matrix products, arithmetic and copies ran while one was open for 19% of the time, Pallas kernels for 0%

commit v1 on v0

v1 whole, which is shorter than its diff:
```python
import numpy as np
import jax
import jax.numpy as jnp
from jax import lax
from jax.sharding import PartitionSpec as P
from jax.experimental import pallas as pl
from jax.experimental.pallas import tpu as pltpu

MESH = pl.DeviceIdType.MESH
BF = jnp.bfloat16
F32 = jnp.float32
D = 4096
HALF = 384
TOK = 24
TOP = 8
CAP = 6
RING = 4
SLOTS = 16 * CAP
CLASS = RING * SLOTS
ROWS = 2 * CLASS
BLOCK = 2 * TOK
PLANE = 16 * BLOCK
LINE = 4 * BLOCK
STEP = 512
X, Y, Z = 0, 1, 2
ORDERS = ((Z, Y, X), (X, Z, Y), (Y, X, Z))
T_AT, T_HALF = (0, 1536, 2816), (768, 640, 640)
G_AT, G_HALF = (0, 1280, 2816), (640, 768, 640)
T_WIDE = (896, 768, 768)
T_SENT = (768, 640, 768)
BACK = (768, 640, 768)


def place_tables():
    i = np.arange(CLASS)
    x, y, z, r = i // 96, i // 24 % 4, i // 6 % 4, i % 6
    rows = (y * 96 + (z * 4 + x) * 6 + r, z * 96 + (x * 4 + y) * 6 + r)
    perm = np.stack([(np.arange(CLASS)[None, :] == w[:, None]) for w in rows]).astype(np.float32)
    k = np.arange(PLANE)
    seg = np.stack([k // BLOCK * CAP, k % BLOCK // TOK]).astype(np.float32)
    return perm, seg


PERM, SEG = place_tables()


def position():
    dp, ex = lax.axis_index("dp"), lax.axis_index("expert")
    return (lax.rem(ex // 2, 4), ex // 8, dp), lax.rem(ex, 2)


def device(co, core):
    return (co[2], co[1] * 8 + co[0] * 2 + core)


def shifted(co, axis, by):
    out = list(co)
    out[axis] = lax.rem(co[axis] + by, RING)
    return tuple(out)


def enter(co, core):
    barrier = pltpu.get_barrier_semaphore()
    for axis in (X, Y, Z):
        for by in (1, 2, 3):
            pl.semaphore_signal(
                barrier, inc=1, device_id=device(shifted(co, axis, by), core), device_id_type=MESH
            )
    pl.semaphore_signal(barrier, inc=1, device_id=device(co, 1 - core), device_id_type=MESH)
    pl.semaphore_wait(barrier, 10)


def remote(src, dst, send, recv, to):
    return pltpu.make_async_remote_copy(
        src_ref=src, dst_ref=dst, send_sem=send, recv_sem=recv, device_id=to, device_id_type=MESH
    )


def expert_of(co):
    return co[2] * 16 + co[1] * 4 + co[0]


def rows_at(start, size):
    return pl.ds(pl.multiple_of(start, 16), size)


def dot(a, b, over=((1,), (0,))):
    return lax.dot_general(a, b, (over, ((), ())), preferred_element_type=F32)


def routing_tile(routes, probs):
    lane = lax.broadcasted_iota(jnp.int32, (TOK, 128), 1)
    named = jnp.zeros((TOK, 128), F32)
    weight = jnp.zeros((TOK, 128), F32)
    for k in range(TOP):
        route = routes[:, k:k + 1]
        named = named + jnp.where(lane == route, 1.0, 0.0)
        weight = weight + jnp.where(lane == route + 64, probs[:, k:k + 1].astype(F32), 0.0)
    before = lax.broadcasted_iota(jnp.int32, (TOK, TOK), 0) > lax.broadcasted_iota(
        jnp.int32, (TOK, TOK), 1
    )
    rank = dot(jnp.where(before, 1.0, 0.0), named)
    meta = named * (rank + 1.0) + weight
    return jnp.concatenate([meta, meta], axis=0).astype(BF)


def kernel(
    tok, grd, routes, probs, perm, perm_t, seg_row, seg_col, gate_w, up_w, down_w,
    token_grad, prob_grad, gate_out, up_out, down_out,
    rows_t, rows_g, wgu, wd,
    gt0, gt1, gt2, gg0, gg1, gg2, st0, st1, st2, sg0, sg1, sg2, rt0, rt1, rt2, rg0, rg1, rg2,
    pk, meta2, other0, other1, other2, rr0, rr1, rr2, bs0, bs1, bs2, us0, us1, us2, cs0, cs1, cs2,
    gu, delta, hid, pp, stage_gu, stage_d,
    a1_s, a1_r, a2_s, a2_r, x_s, x_r, d_s, d_r, m_s, m_r, h_s, h_r,
    y_s, y_r, b2_s, b2_r, b1_s, b1_r, l_s, o_s,
):
    co, core = position()
    partner = device(co, 1 - core)
    gts, ggs = (gt0, gt1, gt2), (gg0, gg1, gg2)
    gat = (gts, ggs)
    sel = ((st0, st1, st2), (sg0, sg1, sg2))
    rec = ((rt0, rt1, rt2), (rg0, rg1, rg2))
    others, rrs, bss = (other0, other1, other2), (rr0, rr1, rr2), (bs0, bs1, bs2)
    uss, css = (us0, us1, us2), (cs0, cs1, cs2)
    at_of, half_of = (T_AT, G_AT), (T_HALF, G_HALF)
    gat_wide = (T_WIDE, G_HALF)
    sent = (T_SENT, G_HALF)
    outs = []

    def send(src, dst, s, r, to):
        c = remote(src, dst, s, r, to)
        c.start()
        outs.append(c)

    def arrive(ref, s, r):
        remote(ref, ref, s, r, partner).wait_recv()

    loads = [
        pltpu.make_async_copy(gate_w.at[0], wgu.at[:, 0:HALF], l_s.at[0]),
        pltpu.make_async_copy(up_w.at[0], wgu.at[:, HALF:2 * HALF], l_s.at[1]),
        pltpu.make_async_copy(down_w.at[0], wd, l_s.at[2]),
    ]
    for c in loads:
        c.start()
    meta = routing_tile(routes, probs)
    enter(co, core)

    def own_slot(p):
        a1, a2, a3 = ORDERS[p]
        return rows_at((co[a2] * 4 + co[a1]) * BLOCK, BLOCK)

    for q, src in enumerate((tok, grd)):
        for p, (a1, a2, a3) in enumerate(ORDERS):
            at, h = at_of[q][p], half_of[q][p]
            both = jnp.concatenate(
                [src[:, at:at + h].astype(F32), src[:, at + h:at + 2 * h].astype(F32)], axis=0
            )
            ref = gat[q][p]
            ref[own_slot(p), 0:h] = both.astype(BF)
            if q == 0:
                ref[own_slot(p), h:h + 128] = meta
            wide = gat_wide[q][p]
            for by in (1, 3, 2):
                view = ref.at[own_slot(p), 0:wide]
                send(
                    view, view, a1_s.at[q, p, by - 1], a1_r.at[q, p, by - 1],
                    device(shifted(co, a1, by), core),
                )

    def part_of_line(q, p, b, which):
        return gat[q][p].at[rows_at(b * LINE + which * (LINE // 2), LINE // 2), 0:gat_wide[q][p]]

    def second_own(q):
        for p, (a1, a2, a3) in enumerate(ORDERS):
            for by in (1, 3, 2):
                theirs = rows_at((co[a2] * 4 + lax.rem(co[a1] + 4 - by, 4)) * BLOCK, BLOCK)
                arrive(
                    gat[q][p].at[theirs, 0:gat_wide[q][p]],
                    a1_s.at[q, p, by - 1], a1_r.at[q, p, by - 1],
                )
            up, down = device(shifted(co, a2, 1), core), device(shifted(co, a2, 3), core)
            for idx, which, to in ((0, 0, up), (3, 1, down), (1, 1, up), (4, 0, down)):
                ref = part_of_line(q, p, co[a2], which)
                send(ref, ref, a2_s.at[q, p, idx], a2_r.at[q, p, idx], to)

    def second_pass(q):
        for p, (a1, a2, a3) in enumerate(ORDERS):
            up, down = device(shifted(co, a2, 1), core), device(shifted(co, a2, 3), core)
            for got, idx, by, which, to in ((0, 2, 3, 0, up), (3, 5, 1, 1, down)):
                ref = part_of_line(q, p, lax.rem(co[a2] + by, 4), which)
                arrive(ref, a2_s.at[q, p, got], a2_r.at[q, p, got])
                send(ref, ref, a2_s.at[q, p, idx], a2_r.at[q, p, idx], to)

    def second_wait(q, p):
        a1, a2, a3 = ORDERS[p]
        for idx, by, which in ((1, 3, 1), (4, 1, 0), (2, 2, 0), (5, 2, 1)):
            arrive(
                part_of_line(q, p, lax.rem(co[a2] + by, 4), which),
                a2_s.at[q, p, idx], a2_r.at[q, p, idx],
            )

    def wanted(p):
        a1, a2, a3 = ORDERS[p]
        h = T_HALF[p]
        line = lax.broadcasted_iota(jnp.int32, (8, 128), 0)
        lane = lax.broadcasted_iota(jnp.int32, (8, 128), 1)
        name = jnp.full((8, 128), -1, jnp.int32)
        for by in range(4):
            name = jnp.where(line == by, expert_of(shifted(co, a3, by)), name)
        pick = jnp.where(lane == name, 1.0, 0.0).astype(BF)
        val = dot(pick, gts[p][:, h:h + 128], ((1,), (1,)))
        return jnp.where(val > 0.5, val - 1.0 + seg_row[0:1, :], -1.0)

    slot = lax.broadcasted_iota(jnp.int32, (SLOTS, PLANE), 0).astype(F32)
    top = seg_row[1:2, :] < 0.5

    def choose(q, p, want, by):
        a1, a2, a3 = ORDERS[p]
        row = want[by:by + 1, :]
        pick = jnp.concatenate(
            [
                jnp.where(slot == jnp.where(top, row, -1.0), 1.0, 0.0),
                jnp.where(slot == jnp.where(top, -1.0, row), 1.0, 0.0),
            ],
            axis=0,
        ).astype(BF)
        w = sent[q][p]
        got = dot(pick, gat[q][p][:, 0:w]).astype(BF)
        mine = rows_at(co[a3] * 192, 192)
        if by == 0:
            rec[q][p][mine, 0:w] = got
        else:
            sel[q][p][by - 1] = got
            send(
                sel[q][p].at[by - 1], rec[q][p].at[mine, 0:w],
                x_s.at[q, p, by - 1], x_r.at[q, p, by - 1], device(shifted(co, a3, by), core),
            )

    mine = rows_at(core * CLASS, CLASS)
    theirs = rows_at((1 - core) * CLASS, CLASS)

    def reorder(q, p, out):
        a1, a2, a3 = ORDERS[p]
        w = sent[q][p]
        for by in (1, 3, 2):
            ref = rec[q][p].at[rows_at(lax.rem(co[a3] + 4 - by, 4) * 192, 192), 0:w]
            arrive(ref, x_s.at[q, p, by - 1], x_r.at[q, p, by - 1])
        at, h = at_of[q][p], half_of[q][p]
        for n in range(2):
            full = jnp.concatenate(
                [rec[q][p][b * 192 + n * 96:b * 192 + n * 96 + 96, 0:w] for b in range(4)], axis=0
            )
            if p > 0:
                full = dot(perm[p - 1], full).astype(BF)
            out[mine, at + n * h:at + n * h + h] = full[:, 0:h]
            if q == 0 and p == 2 and n == 0:
                pk[mine, :] = full[:, h:h + 128]
                send(pk.at[mine], pk.at[mine], m_s.at[0], m_r.at[0], partner)
        view = out.at[mine, at:at + 2 * h]
        send(view, view, d_s.at[q, p], d_r.at[q, p], partner)

    def swapped(q, p, out):
        at, h = at_of[q][p], half_of[q][p]
        arrive(out.at[theirs, at:at + 2 * h], d_s.at[q, p], d_r.at[q, p])

    second_own(0)
    second_pass(0)
    second_own(1)
    wants = []
    for p in range(3):
        second_wait(0, p)
        wants.append(wanted(p))
        for by in (1, 3, 2, 0):
            choose(0, p, wants[p], by)
        if p == 0:
            second_pass(1)
    for p in range(3):
        second_wait(1, p)
        for by in (1, 3, 2, 0):
            choose(1, p, wants[p], by)
    meta2[...] = gts[2][:, 640:768]
    for p in range(3):
        reorder(0, p, rows_t)
    for c in loads:
        c.wait()
    gu[mine, :] = dot(rows_t[mine, :], wgu[...])
    for p in range(3):
        swapped(0, p, rows_t)
    arrive(pk.at[theirs], m_s.at[0], m_r.at[0])
    gu[theirs, :] = dot(rows_t[theirs, :], wgu[...])
    for p in range(3):
        reorder(1, p, rows_g)

    early = list(outs)
    outs.clear()

    def local_terms(rows):
        gate, up = gu[rows, 0:HALF], gu[rows, HALF:2 * HALF]
        raw = dot(rows_g[rows, :], wd[...], ((1,), (1,)))
        lane = lax.broadcasted_iota(jnp.int32, (CLASS, 128), 1)
        weight = jnp.sum(
            jnp.where(lane == 64 + expert_of(co), pk[rows, :].astype(F32), 0.0),
            axis=1, keepdims=True,
        )
        sig = jax.nn.sigmoid(gate)
        active = gate * sig
        hidden = active * up
        scaled = weight * raw
        delta[rows, 0:HALF] = (scaled * up * sig * (1.0 + gate * (1.0 - sig))).astype(BF)
        delta[rows, HALF:2 * HALF] = (scaled * active).astype(BF)
        hid[rows, :] = (weight * hidden).astype(BF)
        part = jnp.sum(hidden * raw, axis=1, keepdims=True)
        pp[rows, :] = jnp.where(lane == expert_of(co), part, 0.0).astype(BF)

    def input_part(rows, p, out):
        at, h = T_AT[p], T_HALF[p]
        d, tile = delta[rows, :], pp[rows, :]
        if p > 0:
            d = dot(perm_t[p - 1], d).astype(BF)
            if p == 2:
                tile = dot(perm_t[p - 1], tile).astype(BF)
        for n in range(2):
            val = dot(d, wgu[at + n * h:at + n * h + h, :], ((1,), (1,))).astype(BF)
            if p == 2:
                val = jnp.concatenate([val, tile if n == 0 else jnp.zeros_like(tile)], axis=1)
            for b in range(4):
                out[b * 192 + n * 96:b * 192 + n * 96 + 96, 0:BACK[p]] = val[b * 96:b * 96 + 96, :]

    local_terms(mine)
    for p in range(3):
        swapped(1, p, rows_g)
    local_terms(theirs)
    away = (rg1, rg0, rg2)
    for p in range(3):
        w = BACK[p]
        input_part(theirs, p, away[p])
        send(away[p].at[:, 0:w], others[p], h_s.at[p], h_r.at[p], partner)
    for p, (a1, a2, a3) in enumerate(ORDERS):
        input_part(mine, p, rec[0][p])
        arrive(others[p], h_s.at[p], h_r.at[p])
        ref = rec[0][p]
        total = ref[...].astype(F32) + others[p][...].astype(F32)
        if p < 2:
            ref[...] = total.astype(BF)
        else:
            ref[:, 0:640] = total[:, 0:640].astype(BF)
            for b in range(4):
                tile = total[b * 192:b * 192 + 96, 640:768]
                hi = tile.astype(BF)
                ref[b * 192:b * 192 + 96, 640:768] = hi
                ref[b * 192 + 96:b * 192 + 192, 640:768] = (tile - hi.astype(F32)).astype(BF)
        for by in (1, 3, 2):
            to = shifted(co, a3, by)
            send(
                ref.at[rows_at(to[a3] * 192, 192)], rrs[p].at[rows_at(co[a3] * 192, 192)],
                y_s.at[p, by - 1], y_r.at[p, by - 1], device(to, core),
            )
        rrs[p][rows_at(co[a3] * 192, 192), :] = ref[rows_at(co[a3] * 192, 192), :]

    def down_step(i, carry):
        for n in range(2):
            @pl.when(i > 0)
            def _():
                pltpu.make_async_copy(
                    stage_d.at[n], down_out.at[0, :, 0:STEP], o_s.at[n]
                ).wait()
            cols = pl.ds(pl.multiple_of((2 * i + n) * STEP, STEP), STEP)
            stage_d[n] = dot(hid[...], rows_g[:, cols], ((0,), (0,))).astype(BF)
            pltpu.make_async_copy(stage_d.at[n], down_out.at[0, :, cols], o_s.at[n]).start()
        return carry

    def gate_up_step(i, carry):
        for n in range(2):
            @pl.when(i > 0)
            def _():
                for m, out in enumerate((gate_out, up_out)):
                    pltpu.make_async_copy(
                        stage_gu.at[n, :, m * HALF:m * HALF + HALF], out.at[0, 0:STEP, :],
                        o_s.at[2 + 2 * n + m],
                    ).wait()
            cols = pl.ds(pl.multiple_of((2 * i + n) * STEP, STEP), STEP)
            stage_gu[n] = dot(rows_t[:, cols], delta[...], ((0,), (0,))).astype(BF)
            for m, out in enumerate((gate_out, up_out)):
                pltpu.make_async_copy(
                    stage_gu.at[n, :, m * HALF:m * HALF + HALF], out.at[0, cols, :],
                    o_s.at[2 + 2 * n + m],
                ).start()
        return carry

    lax.fori_loop(0, 4, down_step, 0)

    for c in early:
        c.wait_send()
    code = lax.broadcasted_iota(jnp.int32, (PLANE, PLANE), 1).astype(F32)
    sums = gts
    for p, (a1, a2, a3) in enumerate(ORDERS):
        w = BACK[p]
        line = lax.broadcasted_iota(jnp.int32, (128, 128), 0)
        lane = lax.broadcasted_iota(jnp.int32, (128, 128), 1)
        name = jnp.full((128, 128), -1, jnp.int32)
        for b in range(4):
            at_b = list(co)
            at_b[a3] = b
            name = jnp.where(line == b, expert_of(at_b), name)
        pick = jnp.where(lane == name, 1.0, 0.0).astype(BF)
        tile = meta2[...] if p == 2 else gts[p][:, T_HALF[p]:T_HALF[p] + 128]
        val = dot(tile, pick, ((1,), (1,)))
        lane = lax.broadcasted_iota(jnp.int32, (PLANE, 128), 1).astype(F32)
        spot = jnp.where(
            val > 0.5, val - 1.0 + seg_col[0] + lane * 192.0 + seg_col[1] * 96.0, -1.0
        )
        put = jnp.zeros((PLANE, PLANE), F32)
        for b in range(4):
            put = jnp.where(code == spot[:, b:b + 1], 1.0, put)
        put = put.astype(BF)
        for by in (1, 3, 2):
            ref = rrs[p].at[rows_at(lax.rem(co[a3] + 4 - by, 4) * 192, 192)]
            arrive(ref, y_s.at[p, by - 1], y_r.at[p, by - 1])
        sums[p][:, 0:w] = dot(put, rrs[p][...]).astype(BF)
        for by in (1, 3, 2):
            to = shifted(co, a2, by)
            send(
                sums[p].at[rows_at(to[a2] * LINE, LINE), 0:w], bss[p].at[by - 1],
                b2_s.at[p, by - 1], b2_r.at[p, by - 1], device(to, core),
            )
    lax.fori_loop(0, 4, gate_up_step, 0)
    for p, (a1, a2, a3) in enumerate(ORDERS):
        total = sums[p][rows_at(co[a2] * LINE, LINE), 0:BACK[p]].astype(F32)
        for by in (1, 3, 2):
            arrive(bss[p].at[by - 1], b2_s.at[p, by - 1], b2_r.at[p, by - 1])
            total = total + bss[p][by - 1].astype(F32)
        uss[p][...] = total.astype(BF)
        for by in (1, 3, 2):
            to = shifted(co, a1, by)
            send(
                uss[p].at[rows_at(to[a1] * BLOCK, BLOCK)], css[p].at[by - 1],
                b1_s.at[p, by - 1], b1_r.at[p, by - 1], device(to, core),
            )
    for p, (a1, a2, a3) in enumerate(ORDERS):
        total = uss[p][rows_at(co[a1] * BLOCK, BLOCK), :].astype(F32)
        for by in (1, 3, 2):
            arrive(css[p].at[by - 1], b1_s.at[p, by - 1], b1_r.at[p, by - 1])
            total = total + css[p][by - 1].astype(F32)
        at, h = T_AT[p], T_HALF[p]
        token_grad[:, at:at + h] = total[0:TOK, 0:h].astype(BF)
        token_grad[:, at + h:at + 2 * h] = total[TOK:, 0:h].astype(BF)
        if p == 2:
            per = total[0:TOK, h:h + 128] + total[TOK:, h:h + 128]
            lane = lax.broadcasted_iota(jnp.int32, (TOK, 128), 1)
            spot = lax.broadcasted_iota(jnp.int32, (TOK, TOP), 1)
            grad = jnp.zeros((TOK, TOP), F32)
            for k in range(TOP):
                one = jnp.sum(jnp.where(lane == routes[:, k:k + 1], per, 0.0), axis=1, keepdims=True)
                grad = jnp.where(spot == k, one, grad)
            prob_grad[...] = grad
    for n in range(2):
        pltpu.make_async_copy(stage_d.at[n], down_out.at[0, :, 0:STEP], o_s.at[n]).wait()
        for m, out in enumerate((gate_out, up_out)):
            pltpu.make_async_copy(
                stage_gu.at[n, :, m * HALF:m * HALF + HALF], out.at[0, 0:STEP, :],
                o_s.at[2 + 2 * n + m],
            ).wait()
    for c in outs:
        c.wait_send()


def on_device(tokens, out_grad, routes, gate_probs, gate_weight, up_weight, down_weight):
    vmem = pl.BlockSpec(memory_space=pltpu.VMEM)
    anywhere = pl.BlockSpec(memory_space=pl.ANY)
    dma = pltpu.SemaphoreType.DMA
    seg = jnp.asarray(SEG, F32)
    shapes = [(ROWS, D), (ROWS, D), (D, 2 * HALF), (HALF, D)]
    shapes += [(PLANE, 896), (PLANE, 768), (PLANE, 768)] + [(PLANE, w) for w in G_HALF]
    shapes += [(3, 192, w) for w in T_SENT] + [(3, 192, w) for w in G_HALF]
    shapes += [(ROWS, w) for w in T_SENT] + [(ROWS, w) for w in (640, 768, 768)]
    shapes += [(ROWS, 128), (PLANE, 128)]
    shapes += [(ROWS, w) for w in BACK] * 2
    shapes += [(3, LINE, w) for w in BACK] + [(LINE, w) for w in BACK]
    shapes += [(3, BLOCK, w) for w in BACK]
    scratch = [pltpu.VMEM(s, BF) for s in shapes]
    scratch += [
        pltpu.VMEM((ROWS, 2 * HALF), F32), pltpu.VMEM((ROWS, 2 * HALF), BF),
        pltpu.VMEM((ROWS, HALF), BF), pltpu.VMEM((ROWS, 128), BF),
        pltpu.VMEM((2, STEP, 2 * HALF), BF), pltpu.VMEM((2, HALF, STEP), BF),
    ]
    for s in ((2, 3, 3), (2, 3, 6), (2, 3, 3), (2, 3), (1,), (3,), (3, 3), (3, 3), (3, 3)):
        scratch += [dma(s), dma(s)]
    scratch += [dma((3,)), dma((6,))]
    return pl.pallas_call(
        kernel,
        out_shape=(
            jax.ShapeDtypeStruct((TOK, D), BF),
            jax.ShapeDtypeStruct((TOK, TOP), F32),
            jax.ShapeDtypeStruct((1, D, HALF), BF),
            jax.ShapeDtypeStruct((1, D, HALF), BF),
            jax.ShapeDtypeStruct((1, HALF, D), BF),
        ),
        in_specs=[vmem] * 8 + [anywhere] * 3,
        out_specs=(vmem, vmem, anywhere, anywhere, anywhere),
        scratch_shapes=scratch,
        compiler_params=pltpu.CompilerParams(
            collective_id=1, has_side_effects=True, vmem_limit_bytes=63 * 2**20
        ),
        name="routed_backward",
    )(
        tokens, out_grad, routes, gate_probs,
        jnp.asarray(PERM, BF), jnp.asarray(PERM.transpose(0, 2, 1), BF),
        seg, jnp.broadcast_to(seg[:, :, None], (2, PLANE, 128)),
        gate_weight, up_weight, down_weight,
    )


def solution(mesh):
    two, three = P(("dp", "expert"), None), P(("dp", "expert"), None, None)
    return jax.shard_map(
        on_device,
        mesh=mesh,
        in_specs=(two, two, two, two, three, three, three),
        out_specs=(two, two, three, three, three),
        check_vma=False,
    )
```

time: 455 us -> 136 us (0.30); the launches traced: 450 us -> 136 us
  waiting for transfers between devices: 243 us -> 0 us
  Pallas kernels: 0 us -> 119 us
  matrix products: 68.4 us -> 0 us
  starting transfers between devices: 58.7 us -> 0 us
  local copies, waits for them, and re-layouts: 67.7 us -> 16.2 us
  other arithmetic: 10.9 us -> 0 us
    all_to_all x5 -> x0, waiting for transfers between devices: 243 us -> none  [the longest x1 90.1 us: on_device(): lax.all_to_all(pair_copies(sent_rows, expert_count, capacity), ('dp', 'ex...]
    pallas_call x0 -> x1, Pallas kernels: none -> 119 us  [on_device(): pl.pallas_call(kernel, out_shape=(jax.ShapeDtypeStruct((TOK, D), BF), jax...]
    dot_general x13 -> x0, matrix products: 68.4 us -> none  [the longest x1 8.42 us: half_terms(): lax.dot_general(grads_in, down_half, (((1,), (1,)), ((), ())), preferred_...]
    all_to_all x5 -> x0, starting transfers between devices: 58.7 us -> none  [the longest x1 14 us: on_device(): lax.all_to_all(pair_copies(sent_grads, expert_count, capacity), ('dp', 'e...]
    reshape x6 -> x0, local copies, waits for them, and re-layouts: 38.9 us -> none  [the longest x1 10.3 us: on_device(): grads_in = got_grads.reshape(-1, model_width)]
    broadcast_in_dim x6 -> x1, local copies, waits for them, and re-layouts: 24.4 us -> 1.84 us  [on_device(): jnp.broadcast_to(seg[:, :, None], (2, PLANE, 128))]
    unnamed x28 -> x10, local copies, waits for them, and re-layouts: 1.74 us -> 13 us
    reduce_sum x4 -> x0, other arithmetic: 9.86 us -> none  [the longest x1 9.57 us: on_device(): jnp.sum(back_input.reshape(expert_count, 2, capacity, model_width).astype...]
  transfers between devices with their start and end apart: 5 -> 0, of which waited for: 3 -> 0; matrix products, arithmetic and copies ran while one was open for 19% -> 0% of each run, Pallas kernels for 0% -> 0%
where the time goes in v1:
time: 136 us
  Pallas kernels  119 us (88%)
  local copies, waits for them, and re-layouts  16.2 us (12%)
    pallas_call x1, Pallas kernels, on_device(): pl.pallas_call(kernel, out_shape=(jax.ShapeDtypeStruct((TOK, D), BF), jax...  119 us
    unnamed x10, local copies, waits for them, and re-layouts  13 us

profile of v1, /device:TPU:0, one launch (start us, length us, event | category | flops | bytes accessed | tf_op | source)
XLA Modules:
  0.0 135.5 jit_solution(17859335570788421130)
XLA Ops:
  0.6 1.3 copy.16.probs
  2.0 1.4 %copy.15.routes = s32[24,8]{1,0:T(8,128)} copy(s32[24,8]{0,1:T(8,128)} %param.12) | data formatting | bytes 1536 | tf_op args[2]
  3.3 1.8 %broadcast_in_dim.2.seg_col = f32[2,768,128]{2,1,0:T(8,128)} broadcast(f32[2,768]{1,0:T(2,128)} %constant.6.clone.seg_row), dimensions={0,1} | broadcast | bytes 792576 | tf_op jit(solution)/shard_map/broadcast_in_dim | solution.py:508
  5.2 118.7 %routed_backward.1 = (bf16[24,4096]{1,0:T(8,128)(2,1)}, f32[24,8]{1,0:T(8,128)}, bf16[1,4096,384]{2,1,0:T(8,128)(2,1)}, bf16[1,4096,384]{2,1,0:T(8,128)(2,1)}, bf16[1,384,4096]{2,1,0:T(8,128)(2,1)}) custom-call(bf16[24,4096]{1,0:T(8,128)(2,1)} %tok.1, bf16[24,4096]{1,0:T(8,128)(2,1)} %grd.1, s32[24,8]{1,0:T(8,128)} %copy.15.routes, ...), custom_call_target="tpu_custom_call" | custom-call | tf_op jit(solution)/shard_map/routed_backward/pallas_call | solution.py:489
  123.8 1.4 %copy.17 = f32[24,8]{0,1:T(8,128)} copy(f32[24,8]{1,0:T(8,128)} %get-tuple-element.6) | data formatting | bytes 1536 | tf_op jit(solution)/shard_map/routed_backward/pallas_call | solution.py:489
  125.2 1.6 %copy.22 = bf16[24,4096]{1,0:T(8,128)(2,1)} copy(bf16[24,4096]{1,0:T(8,128)(2,1)} %get-tuple-element.15) | data formatting | bytes 393216
  126.8 0.0 copy-start.1
  126.8 4.0 %copy.23 = bf16[1,4096,384]{2,1,0:T(8,128)(2,1)} copy(bf16[1,4096,384]{2,1,0:T(8,128)(2,1)} %get-tuple-element.17) | data formatting | bytes 6291456
  130.8 0.0 copy-done.1
  130.9 0.0 copy-start
  130.9 1.7 %copy.24 = bf16[1,4096,384]{2,1,0:T(8,128)(2,1)} copy(bf16[1,4096,384]{2,1,0:T(8,128)(2,1)S(1)} %copy-done.1) | data formatting | bytes 6291456
  132.5 1.4 %copy-done = bf16[1,384,4096]{2,1,0:T(8,128)(2,1)S(1)} copy-done((bf16[1,384,4096]{2,1,0:T(8,128)(2,1)S(1)}, bf16[1,384,4096]{2,1,0:T(8,128)(2,1)}, u32[]{:S(2)}) %copy-start) | copy-done | bytes 3145752
  133.9 1.7 %copy.25 = bf16[1,384,4096]{2,1,0:T(8,128)(2,1)} copy(bf16[1,384,4096]{2,1,0:T(8,128)(2,1)S(1)} %copy-done) | data formatting | bytes 6291456
Async XLA Ops:
  126.8 4.0 %copy-start.1 = (bf16[1,4096,384]{2,1,0:T(8,128)(2,1)S(1)}, bf16[1,4096,384]{2,1,0:T(8,128)(2,1)}, u32[]{:S(2)}) copy-start(bf16[1,4096,384]{2,1,0:T(8,128)(2,1)} %get-tuple-element.18) | copy-start | bytes 9437188
  130.9 3.0 %copy-start = (bf16[1,384,4096]{2,1,0:T(8,128)(2,1)S(1)}, bf16[1,384,4096]{2,1,0:T(8,128)(2,1)}, u32[]{:S(2)}) copy-start(bf16[1,384,4096]{2,1,0:T(8,128)(2,1)} %get-tuple-element.19) | copy-start | bytes 9437188

commit v2 on v1

v2 whole, which is shorter than its diff:
```python
import numpy as np
import jax
import jax.numpy as jnp
from jax import lax
from jax.sharding import PartitionSpec as P
from jax.experimental import pallas as pl
from jax.experimental.pallas import tpu as pltpu

MESH = pl.DeviceIdType.MESH
BF = jnp.bfloat16
F32 = jnp.float32
D = 4096
HALF = 384
TOK = 24
TOP = 8
CAP = 6
RING = 4
SLOTS = 16 * CAP
CLASS = RING * SLOTS
ROWS = 2 * CLASS
BLOCK = 2 * TOK
PLANE = 16 * BLOCK
LINE = 4 * BLOCK
STEP = 256
X, Y, Z = 0, 1, 2
ORDERS = ((Z, Y, X), (X, Z, Y), (Y, X, Z))
T_AT, T_HALF = (0, 1536, 2816), (768, 640, 640)
G_AT, G_HALF = (0, 1280, 2816), (640, 768, 640)
T_WIDE = (896, 768, 768)
T_SENT = (768, 640, 768)
BACK = (768, 640, 768)
CUT = 384


def place_tables():
    i = np.arange(CLASS)
    x, y, z, r = i // 96, i // 24 % 4, i // 6 % 4, i % 6
    rows = (y * 96 + (z * 4 + x) * 6 + r, z * 96 + (x * 4 + y) * 6 + r)
    perm = np.stack([(np.arange(CLASS)[None, :] == w[:, None]) for w in rows]).astype(np.float32)
    return perm


PERM = place_tables()


def position():
    dp, ex = lax.axis_index("dp"), lax.axis_index("expert")
    return (lax.rem(ex // 2, 4), ex // 8, dp), lax.rem(ex, 2)


def device(co, core):
    return (co[2], co[1] * 8 + co[0] * 2 + core)


def shifted(co, axis, by):
    out = list(co)
    out[axis] = lax.rem(co[axis] + by, RING)
    return tuple(out)


def enter(co, core):
    barrier = pltpu.get_barrier_semaphore()
    for axis in (X, Y, Z):
        for by in (1, 2, 3):
            pl.semaphore_signal(
                barrier, inc=1, device_id=device(shifted(co, axis, by), core), device_id_type=MESH
            )
    pl.semaphore_signal(barrier, inc=1, device_id=device(co, 1 - core), device_id_type=MESH)
    pl.semaphore_wait(barrier, 10)


def remote(src, dst, send, recv, to):
    return pltpu.make_async_remote_copy(
        src_ref=src, dst_ref=dst, send_sem=send, recv_sem=recv, device_id=to, device_id_type=MESH
    )


def expert_of(co):
    return co[2] * 16 + co[1] * 4 + co[0]


def rows_at(start, size):
    return pl.ds(pl.multiple_of(start, 16), size)


def dot(a, b, over=((1,), (0,))):
    return lax.dot_general(a, b, (over, ((), ())), preferred_element_type=F32)


def segment(k):
    place = jnp.floor((k + 0.5) * (1.0 / BLOCK))
    half = jnp.where(k - place * BLOCK > TOK - 0.5, 1.0, 0.0)
    return place * CAP, half


def unit(n, dtype):
    return jnp.where(
        lax.broadcasted_iota(jnp.int32, (n, n), 0) == lax.broadcasted_iota(jnp.int32, (n, n), 1),
        1.0, 0.0,
    ).astype(dtype)


def routing_tile(routes, probs):
    lane = lax.broadcasted_iota(jnp.int32, (TOK, 128), 1).astype(F32)
    named = jnp.zeros((TOK, 128), F32)
    weight = jnp.zeros((TOK, 128), F32)
    for k in range(TOP):
        route = routes[:, k:k + 1]
        named = named + jnp.where(lane == route, 1.0, 0.0)
        weight = weight + jnp.where(lane == route + 64.0, probs[:, k:k + 1], 0.0)
    before = lax.broadcasted_iota(jnp.int32, (TOK, TOK), 0) > lax.broadcasted_iota(
        jnp.int32, (TOK, TOK), 1
    )
    rank = dot(jnp.where(before, 1.0, 0.0), named)
    meta = named * (rank + 1.0) + weight
    return jnp.concatenate([meta, meta], axis=0).astype(BF)


def kernel(
    tok, grd, routes_in, probs_in, perm_in, gate_w, up_w, down_w,
    token_grad, prob_grad, gate_out, up_out, down_out,
    rows_t, rows_g, wgu, wd,
    gt0, gt1, gt2, gg0, gg1, gg2, st0, st1, st2, sg0, sg1, sg2, rt0, rt1, rt2, rg0, rg1, rg2,
    rr0, rr1, rr2, bs0, bs1, bs2, cs0, cs1, cs2,
    perm, delta, hid, gu,
    a1_s, a1_r, a2_s, a2_r, x_s, x_r, d_s, d_r, w_s, w_r, h_s, h_r,
    y_s, y_r, b2_s, b2_r, b1_s, b1_r, l_s, o_s,
):
    co, core = position()
    partner = device(co, 1 - core)
    gts, ggs = (gt0, gt1, gt2), (gg0, gg1, gg2)
    gat = (gts, ggs)
    sel = ((st0, st1, st2), (sg0, sg1, sg2))
    rec = ((rt0, rt1, rt2), (rg0, rg1, rg2))
    rrs, bss = (rr0, rr1, rr2), (bs0, bs1, bs2)
    css = (cs0, cs1, cs2)
    delta_o, hid_o, ptile = st0.at[0:CLASS], st2.at[0:CLASS, 0:HALF], st1.at[0:CLASS, 0:256]
    pk = gt0.at[0:CLASS, 768:896]
    uss = (st0.at[CLASS:576], st1.at[CLASS:576], st2.at[CLASS:576])
    at_of, half_of = (T_AT, G_AT), (T_HALF, G_HALF)
    gat_wide = (T_WIDE, G_HALF)
    sent = (T_SENT, G_HALF)
    outs = []

    def send(src, dst, s, r, to):
        c = remote(src, dst, s, r, to)
        c.start()
        outs.append(c)

    def arrive(ref, s, r):
        remote(ref, ref, s, r, partner).wait_recv()

    def settle():
        for c in outs:
            c.wait_send()
        outs.clear()

    H2 = 2 * HALF
    loads = [
        pltpu.make_async_copy(gate_w.at[0], wgu.at[:, 0:HALF], l_s.at[0]),
        pltpu.make_async_copy(up_w.at[0], wgu.at[:, HALF:H2], l_s.at[1]),
        pltpu.make_async_copy(down_w.at[0], wd.at[0:HALF], l_s.at[2]),
        pltpu.make_async_copy(perm_in, perm, l_s.at[3]),
    ]
    for c in loads:
        c.start()
    eye = unit(TOK, F32)
    routes = dot(eye, routes_in[...].astype(F32), ((1,), (1,)))
    meta = routing_tile(routes, dot(eye, probs_in[...].astype(F32), ((1,), (1,))))

    def own_slot(p):
        a1, a2, a3 = ORDERS[p]
        return rows_at((co[a2] * 4 + co[a1]) * BLOCK, BLOCK)

    def pack(q, src):
        for p in range(3):
            at, h = at_of[q][p], half_of[q][p]
            both = jnp.concatenate(
                [src[:, at:at + h].astype(F32), src[:, at + h:at + 2 * h].astype(F32)], axis=0
            )
            gat[q][p][own_slot(p), 0:h] = both.astype(BF)
            if q == 0:
                gat[q][p][own_slot(p), h:h + 128] = meta

    def first(q):
        for p, (a1, a2, a3) in enumerate(ORDERS):
            view = gat[q][p].at[own_slot(p), 0:gat_wide[q][p]]
            for by in (1, 3, 2):
                send(
                    view, view, a1_s.at[q, p, by - 1], a1_r.at[q, p, by - 1],
                    device(shifted(co, a1, by), core),
                )

    pack(0, tok)
    enter(co, core)
    first(0)
    pack(1, grd)
    first(1)
    gathered = list(outs)
    outs.clear()
    send(gate_w.at[0], wgu.at[:, H2:H2 + HALF], w_s.at[0], w_r.at[0], partner)
    send(up_w.at[0], wgu.at[:, H2 + HALF:2 * H2], w_s.at[1], w_r.at[1], partner)
    send(down_w.at[0], wd.at[HALF:H2], w_s.at[2], w_r.at[2], partner)
    weights = list(outs)
    outs.clear()

    def part_of_line(q, p, b, which):
        return gat[q][p].at[rows_at(b * LINE + which * (LINE // 2), LINE // 2), 0:gat_wide[q][p]]

    def second_own(q):
        for p, (a1, a2, a3) in enumerate(ORDERS):
            for by in (1, 3, 2):
                theirs = rows_at((co[a2] * 4 + lax.rem(co[a1] + 4 - by, 4)) * BLOCK, BLOCK)
                arrive(
                    gat[q][p].at[theirs, 0:gat_wide[q][p]],
                    a1_s.at[q, p, by - 1], a1_r.at[q, p, by - 1],
                )
            up, down = device(shifted(co, a2, 1), core), device(shifted(co, a2, 3), core)
            for idx, which, to in ((0, 0, up), (3, 1, down), (1, 1, up), (4, 0, down)):
                ref = part_of_line(q, p, co[a2], which)
                send(ref, ref, a2_s.at[q, p, idx], a2_r.at[q, p, idx], to)
                gathered.append(outs.pop())

    def second_pass(q):
        for p, (a1, a2, a3) in enumerate(ORDERS):
            up, down = device(shifted(co, a2, 1), core), device(shifted(co, a2, 3), core)
            for got, idx, by, which, to in ((0, 2, 3, 0, up), (3, 5, 1, 1, down)):
                ref = part_of_line(q, p, lax.rem(co[a2] + by, 4), which)
                arrive(ref, a2_s.at[q, p, got], a2_r.at[q, p, got])
                send(ref, ref, a2_s.at[q, p, idx], a2_r.at[q, p, idx], to)
                gathered.append(outs.pop())

    def second_wait(q, p):
        a1, a2, a3 = ORDERS[p]
        for idx, by, which in ((1, 3, 1), (4, 1, 0), (2, 2, 0), (5, 2, 1)):
            arrive(
                part_of_line(q, p, lax.rem(co[a2] + by, 4), which),
                a2_s.at[q, p, idx], a2_r.at[q, p, idx],
            )

    k_row = lax.broadcasted_iota(jnp.int32, (1, PLANE), 1).astype(F32)
    place_row, half_row = segment(k_row)
    top = half_row < 0.5
    slot = lax.broadcasted_iota(jnp.int32, (SLOTS, PLANE), 0).astype(F32)

    def wanted(p):
        a1, a2, a3 = ORDERS[p]
        h = T_HALF[p]
        line = lax.broadcasted_iota(jnp.int32, (8, 128), 0)
        lane = lax.broadcasted_iota(jnp.int32, (8, 128), 1)
        name = jnp.full((8, 128), -1, jnp.int32)
        for by in range(4):
            name = jnp.where(line == by, expert_of(shifted(co, a3, by)), name)
        pick = jnp.where(lane == name, 1.0, 0.0).astype(BF)
        val = dot(pick, gts[p][:, h:h + 128], ((1,), (1,)))
        return jnp.where(val > 0.5, val - 1.0 + place_row, -1.0)

    def choose(q, p, want):
        a1, a2, a3 = ORDERS[p]
        picks = []
        for by in (1, 3, 2, 0):
            row = want[by:by + 1, :]
            picks.append(jnp.where(slot == jnp.where(top, row, -1.0), 1.0, 0.0).astype(BF))
            picks.append(jnp.where(slot == jnp.where(top, -1.0, row), 1.0, 0.0).astype(BF))
        w = sent[q][p]
        got = dot(jnp.concatenate(picks, axis=0), gat[q][p][:, 0:w]).astype(BF)
        mine = rows_at(co[a3] * 192, 192)
        for n, by in enumerate((1, 3, 2)):
            rows = slice(n * 192, n * 192 + 192)
            sel[q][p][rows, :] = got[rows]
            send(
                sel[q][p].at[rows], rec[q][p].at[mine, 0:w],
                x_s.at[q, p, by - 1], x_r.at[q, p, by - 1], device(shifted(co, a3, by), core),
            )
        rec[q][p][mine, 0:w] = got[576:768]

    def reorder(q, p, out):
        a1, a2, a3 = ORDERS[p]
        w = sent[q][p]
        for by in (1, 3, 2):
            ref = rec[q][p].at[rows_at(lax.rem(co[a3] + 4 - by, 4) * 192, 192), 0:w]
            arrive(ref, x_s.at[q, p, by - 1], x_r.at[q, p, by - 1])
        at, h = at_of[q][p], half_of[q][p]
        for n in range(2):
            full = jnp.concatenate(
                [rec[q][p][b * 192 + n * 96:b * 192 + n * 96 + 96, 0:w] for b in range(4)], axis=0
            )
            if p > 0:
                full = dot(perm[p - 1], full).astype(BF)
            out[0:CLASS, at + n * h:at + n * h + h] = full[:, 0:h]
            if q == 0 and p == 2 and n == 0:
                pk[...] = full[:, h:h + 128]
        send(
            out.at[0:CLASS, at:at + 2 * h], out.at[CLASS:ROWS, at:at + 2 * h],
            d_s.at[q, p], d_r.at[q, p], partner,
        )

    second_own(0)
    second_pass(0)
    second_own(1)
    wants = []
    for p in range(3):
        second_wait(0, p)
        wants.append(wanted(p))
        choose(0, p, wants[p])
        if p == 0:
            second_pass(1)
    for p in range(3):
        second_wait(1, p)
        choose(1, p, wants[p])
    for c in gathered:
        c.wait_send()
    exchanged = list(outs)
    outs.clear()
    code = lax.broadcasted_iota(jnp.int32, (LINE, PLANE), 1).astype(F32)
    k_col = lax.broadcasted_iota(jnp.int32, (PLANE, 128), 0).astype(F32)
    place_col, half_col = segment(k_col)
    for p, (a1, a2, a3) in enumerate(ORDERS):
        line = lax.broadcasted_iota(jnp.int32, (128, 128), 0)
        lane = lax.broadcasted_iota(jnp.int32, (128, 128), 1)
        name = jnp.full((128, 128), -1, jnp.int32)
        for b in range(4):
            at_b = list(co)
            at_b[a3] = b
            name = jnp.where(line == b, expert_of(at_b), name)
        pick = jnp.where(lane == name, 1.0, 0.0).astype(BF)
        val = dot(gts[p][:, T_HALF[p]:T_HALF[p] + 128], pick, ((1,), (1,)))
        lane = lax.broadcasted_iota(jnp.int32, (PLANE, 128), 1).astype(F32)
        spot = jnp.where(
            val > 0.5, val - 1.0 + place_col + lane * 192.0 + half_col * 96.0, -1.0
        )
        for r in range(0, PLANE, LINE):
            put = jnp.zeros((LINE, PLANE), F32)
            for b in range(4):
                put = jnp.where(code == spot[r:r + LINE, b:b + 1], 1.0, put)
            ggs[p][r:r + LINE, :] = put.astype(BF)
    for c in loads:
        c.wait()
    for p in range(3):
        reorder(0, p, rows_t)
    gu[:, 0:H2] = dot(rows_t[0:CLASS, :], wgu[:, 0:H2])
    arrive(wgu.at[:, H2:H2 + HALF], w_s.at[0], w_r.at[0])
    arrive(wgu.at[:, H2 + HALF:2 * H2], w_s.at[1], w_r.at[1])
    arrive(wd.at[HALF:H2], w_s.at[2], w_r.at[2])
    gu[:, H2:2 * H2] = dot(rows_t[0:CLASS, :], wgu[:, H2:2 * H2])
    for p in range(3):
        reorder(1, p, rows_g)

    for c in exchanged:
        c.wait_send()
    lane = lax.broadcasted_iota(jnp.int32, (CLASS, 128), 1)
    weight = jnp.sum(
        jnp.where(lane == 64 + expert_of(co), pk[...].astype(F32), 0.0), axis=1, keepdims=True
    )
    prob = jnp.zeros((CLASS, 1), F32)
    for n, (dl, hd) in enumerate(((delta, hid), (delta_o, hid_o))):
        gate, up = gu[:, n * H2:n * H2 + HALF], gu[:, n * H2 + HALF:n * H2 + H2]
        grad = dot(rows_g[0:CLASS, :], wd[n * HALF:n * HALF + HALF, :], ((1,), (1,)))
        sig = jax.nn.sigmoid(gate)
        active = gate * sig
        hidden = active * up
        scaled = weight * grad
        dl[0:CLASS, 0:HALF] = (scaled * up * sig * (1.0 + gate * (1.0 - sig))).astype(BF)
        dl[0:CLASS, HALF:H2] = (scaled * active).astype(BF)
        hd[0:CLASS, :] = (weight * hidden).astype(BF)
        prob = prob + jnp.sum(hidden * grad, axis=1, keepdims=True).astype(BF).astype(F32)
    prob = jnp.where(lane == expert_of(co), prob, 0.0)
    prob_hi = prob.astype(BF)
    ptile[:, 0:128] = prob_hi
    ptile[:, 128:256] = (prob - prob_hi.astype(F32)).astype(BF)

    def piece(p, c):
        h = CUT if c == 0 else T_HALF[p] - CUT
        return T_AT[p] + c * 2 * CUT, h, slice(c * CUT, c * CUT + h + (128 if (p, c) == (2, 1) else 0))

    def input_part(p, c):
        a1, a2, a3 = ORDERS[p]
        at, h, cols = piece(p, c)
        if p == 0:
            own, other = delta[0:CLASS, :], delta_o[...]
        else:
            if c == 0:
                rec[1][p][0:CLASS, :] = dot(perm[p - 1], delta[0:CLASS, :], ((0,), (0,))).astype(BF)
                rec[1][p][CLASS:ROWS, :] = dot(perm[p - 1], delta_o[...], ((0,), (0,))).astype(BF)
            own, other = rec[1][p][0:CLASS, :], rec[1][p][CLASS:ROWS, :]
        if (p, c) == (2, 1):
            tiles = dot(perm[p - 1], ptile[...], ((0,), (0,))).astype(BF)
        for n in range(2):
            w = slice(at + n * h, at + n * h + h)
            val = (
                dot(own, wgu[w, 0:H2], ((1,), (1,))) + dot(other, wgu[w, H2:2 * H2], ((1,), (1,)))
            ).astype(BF)
            if (p, c) == (2, 1):
                val = jnp.concatenate([val, tiles[:, n * 128:n * 128 + 128]], axis=1)
            for b in range(4):
                rec[0][p][b * 192 + n * 96:b * 192 + n * 96 + 96, cols] = val[b * 96:b * 96 + 96, :]
        for by in (1, 3, 2):
            to = shifted(co, a3, by)
            send(
                rec[0][p].at[rows_at(to[a3] * 192, 192), cols],
                rrs[p].at[rows_at(co[a3] * 192, 192), cols],
                y_s.at[c, p, by - 1], y_r.at[c, p, by - 1], device(to, core),
            )
        mine = rows_at(co[a3] * 192, 192)
        rrs[p][mine, cols] = rec[0][p][mine, cols]

    for c in range(2):
        for p in range(3):
            input_part(p, c)
    send(delta_o, delta.at[CLASS:ROWS], h_s.at[0], h_r.at[0], partner)
    send(hid_o, hid.at[CLASS:ROWS], h_s.at[1], h_r.at[1], partner)

    stage_d = (rg0.at[0:CLASS, 0:STEP], rg0.at[CLASS:ROWS, 0:STEP])
    stage_gu = (rg1, rg2)

    def down_out_copy(n, cols):
        return pltpu.make_async_copy(stage_d[n], down_out.at[0, :, cols], o_s.at[n])

    def gate_up_copies(n, cols):
        return [
            pltpu.make_async_copy(
                stage_gu[n].at[0:STEP, m * HALF:m * HALF + HALF], out.at[0, cols, :],
                o_s.at[2 + 2 * n + m],
            )
            for m, out in enumerate((gate_out, up_out))
        ]

    def down_step(i, carry):
        for n in range(2):
            @pl.when(i > 0)
            def _():
                down_out_copy(n, slice(0, STEP)).wait()
            cols = pl.ds(pl.multiple_of((2 * i + n) * STEP, STEP), STEP)
            stage_d[n][...] = dot(hid[...], rows_g[:, cols], ((0,), (0,))).astype(BF)
            down_out_copy(n, cols).start()
        return carry

    def gate_up_step(i, carry):
        for n in range(2):
            @pl.when(i > 0)
            def _():
                for c in gate_up_copies(n, slice(0, STEP)):
                    c.wait()
            cols = pl.ds(pl.multiple_of((2 * i + n) * STEP, STEP), STEP)
            stage_gu[n][0:STEP, :] = dot(rows_t[:, cols], delta[...], ((0,), (0,))).astype(BF)
            for c in gate_up_copies(n, cols):
                c.start()
        return carry

    sums = gts

    def relay(c):
        for p, (a1, a2, a3) in enumerate(ORDERS):
            cols = piece(p, c)[2]
            for by in (1, 3, 2):
                ref = rrs[p].at[rows_at(lax.rem(co[a3] + 4 - by, 4) * 192, 192), cols]
                arrive(ref, y_s.at[c, p, by - 1], y_r.at[c, p, by - 1])
            sums[p][:, cols] = dot(ggs[p][...], rrs[p][:, cols]).astype(BF)
            for by in (1, 3, 2):
                to = shifted(co, a2, by)
                send(
                    sums[p].at[rows_at(to[a2] * LINE, LINE), cols], bss[p].at[by - 1, :, cols],
                    b2_s.at[c, p, by - 1], b2_r.at[c, p, by - 1], device(to, core),
                )

    def line_sum(c):
        for p, (a1, a2, a3) in enumerate(ORDERS):
            cols = piece(p, c)[2]
            total = sums[p][rows_at(co[a2] * LINE, LINE), cols].astype(F32)
            for by in (1, 3, 2):
                arrive(bss[p].at[by - 1, :, cols], b2_s.at[c, p, by - 1], b2_r.at[c, p, by - 1])
                total = total + bss[p][by - 1, :, cols].astype(F32)
            uss[p][:, cols] = total.astype(BF)
            for by in (1, 3, 2):
                to = shifted(co, a1, by)
                send(
                    uss[p].at[rows_at(to[a1] * BLOCK, BLOCK), cols], css[p].at[by - 1, :, cols],
                    b1_s.at[c, p, by - 1], b1_r.at[c, p, by - 1], device(to, core),
                )

    def finish(c):
        for p, (a1, a2, a3) in enumerate(ORDERS):
            at, h, cols = piece(p, c)
            total = uss[p][rows_at(co[a1] * BLOCK, BLOCK), cols].astype(F32)
            for by in (1, 3, 2):
                arrive(css[p].at[by - 1, :, cols], b1_s.at[c, p, by - 1], b1_r.at[c, p, by - 1])
                total = total + css[p][by - 1, :, cols].astype(F32)
            token_grad[:, at:at + h] = total[0:TOK, 0:h].astype(BF)
            token_grad[:, at + h:at + 2 * h] = total[TOK:, 0:h].astype(BF)
            if (p, c) == (2, 1):
                per = total[0:TOK, h:h + 128] + total[TOK:, h:h + 128]
                lane = lax.broadcasted_iota(jnp.int32, (TOK, 128), 1).astype(F32)
                spot = lax.broadcasted_iota(jnp.int32, (TOK, TOP), 1)
                grad = jnp.zeros((TOK, TOP), F32)
                for k in range(TOP):
                    one = jnp.sum(
                        jnp.where(lane == routes[:, k:k + 1], per, 0.0), axis=1, keepdims=True
                    )
                    grad = jnp.where(spot == k, one, grad)
                prob_grad[...] = lax.dot_general(
                    unit(TOP, F32), grad, (((1,), (1,)), ((), ())),
                    preferred_element_type=F32, precision=lax.Precision.HIGHEST,
                )

    relay(0)
    for q, out in ((0, rows_t), (1, rows_g)):
        for p in range(3):
            at, h = at_of[q][p], half_of[q][p]
            arrive(out.at[CLASS:ROWS, at:at + 2 * h], d_s.at[q, p], d_r.at[q, p])
    arrive(delta.at[CLASS:ROWS], h_s.at[0], h_r.at[0])
    arrive(hid.at[CLASS:ROWS], h_s.at[1], h_r.at[1])
    lax.fori_loop(0, 8, down_step, 0)
    relay(1)
    line_sum(0)
    lax.fori_loop(0, 6, gate_up_step, 0)
    line_sum(1)
    lax.fori_loop(6, 8, gate_up_step, 0)
    finish(0)
    finish(1)
    for n in range(2):
        down_out_copy(n, slice(0, STEP)).wait()
        for c in gate_up_copies(n, slice(0, STEP)):
            c.wait()
    for c in weights:
        c.wait_send()
    settle()


def emit_kernel(token, prob, gate, up, down, token_out, prob_out, gate_out, up_out, down_out, held, held_d, sems):
    jobs = []
    for n, (src, dst) in enumerate(((gate, gate_out), (up, up_out), (down, down_out))):
        rows = src.shape[1] // 4
        for i in range(4):
            part = slice(i * rows, i * rows + rows)
            mid = held_d.at[part] if n == 2 else held.at[n, part]
            c = pltpu.make_async_copy(src.at[0, part], mid, sems.at[0, n, i])
            c.start()
            jobs.append((c, pltpu.make_async_copy(mid, dst.at[0, part], sems.at[1, n, i])))
    token_out[...] = token[...]
    prob_out[...] = prob[...]
    for c, d in jobs:
        c.wait()
        d.start()
    for c, d in jobs:
        d.wait()


def on_device(tokens, out_grad, routes, gate_probs, gate_weight, up_weight, down_weight):
    vmem = pl.BlockSpec(memory_space=pltpu.VMEM)
    anywhere = pl.BlockSpec(memory_space=pl.ANY)
    dma = pltpu.SemaphoreType.DMA
    shapes = [(ROWS, D), (ROWS, D), (D, 4 * HALF), (2 * HALF, D)]
    shapes += [(PLANE, 896), (PLANE, 768), (PLANE, 768)] + [(PLANE, 768)] * 3
    shapes += [(576, w) for w in T_SENT] + [(576, w) for w in G_HALF]
    shapes += [(ROWS, w) for w in T_SENT] + [(ROWS, w) for w in (640, 768, 768)]
    shapes += [(ROWS, w) for w in BACK]
    shapes += [(3, LINE, w) for w in BACK]
    shapes += [(3, BLOCK, w) for w in BACK]
    shapes += [PERM.shape, (ROWS, 2 * HALF), (ROWS, HALF)]
    scratch = [pltpu.VMEM(s, BF) for s in shapes] + [pltpu.VMEM((CLASS, 4 * HALF), F32)]
    for s in ((2, 3, 3), (2, 3, 6), (2, 3, 3), (2, 3), (3,), (2,)) + ((2, 3, 3),) * 3:
        scratch += [dma(s), dma(s)]
    scratch += [dma((4,)), dma((6,))]
    shaped = (
        jax.ShapeDtypeStruct((TOK, D), BF),
        jax.ShapeDtypeStruct((TOP, TOK), F32),
        jax.ShapeDtypeStruct((1, D, HALF), BF),
        jax.ShapeDtypeStruct((1, D, HALF), BF),
        jax.ShapeDtypeStruct((1, HALF, D), BF),
    )
    results = pl.pallas_call(
        kernel,
        out_shape=shaped,
        in_specs=[vmem] * 4 + [anywhere] * 4,
        out_specs=(vmem, vmem, anywhere, anywhere, anywhere),
        scratch_shapes=scratch,
        compiler_params=pltpu.CompilerParams(
            collective_id=1, has_side_effects=True, vmem_limit_bytes=65400 * 2**10
        ),
        name="routed_backward",
    )(
        tokens, out_grad, routes.T, gate_probs.T, jnp.asarray(PERM, BF),
        gate_weight, up_weight, down_weight,
    )
    token_grad, prob_grad, gate_grad, up_grad, down_grad = pl.pallas_call(
        emit_kernel,
        out_shape=shaped,
        in_specs=[vmem] * 2 + [anywhere] * 3,
        out_specs=(vmem, vmem, anywhere, anywhere, anywhere),
        scratch_shapes=[pltpu.VMEM((2, D, HALF), BF), pltpu.VMEM((HALF, D), BF), dma((2, 3, 4))],
        compiler_params=pltpu.CompilerParams(vmem_limit_bytes=62 * 2**20),
        name="emit",
    )(*results)
    return token_grad, prob_grad.T, gate_grad, up_grad, down_grad


def solution(mesh):
    two, three = P(("dp", "expert"), None), P(("dp", "expert"), None, None)
    return jax.shard_map(
        on_device,
        mesh=mesh,
        in_specs=(two, two, two, two, three, three, three),
        out_specs=(two, two, three, three, three),
        check_vma=False,
    )
```

time: 136 us -> 121 us (0.89)
  local copies, waits for them, and re-layouts: 16.2 us -> 0 us
    unnamed x10 -> x0, local copies, waits for them, and re-layouts: 13 us -> none
    broadcast_in_dim x1 -> x0, local copies, waits for them, and re-layouts: 1.84 us -> none  [on_device(): jnp.broadcast_to(seg[:, :, None], (2, PLANE, 128))]
    pallas_call x1 -> x2, Pallas kernels: 119 us -> 120 us  [the longest x1 111 us: on_device(): pl.pallas_call(kernel, out_shape=shaped, in_specs=[vmem] * 4 + [anywhere]...]
    pallas_call x1 -> x0, local copies, waits for them, and re-layouts: 1.37 us -> none  [on_device(): pl.pallas_call(kernel, out_shape=(jax.ShapeDtypeStruct((TOK, D), BF), jax...]
where the time goes in v2:
time: 121 us
  Pallas kernels  120 us (99%)
    pallas_call x1, Pallas kernels, on_device(): pl.pallas_call(kernel, out_shape=shaped, in_specs=[vmem] * 4 + [anywhere]...  111 us
    pallas_call x1, Pallas kernels, on_device(): pl.pallas_call(emit_kernel, out_shape=shaped, in_specs=[vmem] * 2 + [anyw...  8.88 us

profile of v2, /device:TPU:0, one launch (start us, length us, event | category | flops | bytes accessed | tf_op | source)
XLA Modules:
  0.0 120.9 jit_solution(4502572256299134194)
XLA Ops:
  0.6 111.2 %routed_backward.1 = (bf16[24,4096]{1,0:T(8,128)(2,1)}, f32[8,24]{1,0:T(8,128)}, bf16[1,4096,384]{2,1,0:T(8,128)(2,1)}, bf16[1,4096,384]{2,1,0:T(8,128)(2,1)}, bf16[1,384,4096]{2,1,0:T(8,128)(2,1)}) custom-call(bf16[24,4096]{1,0:T(8,128)(2,1)} %tok.1, bf16[24,4096]{1,0:T(8,128)(2,1)} %grd.1, s32[8,24]{1,0:T(8,128)} %bitcast.3, bf16[8,24]{1,0:T(8,128)(2,1)} %bitcast.4, ...), custom_call_target="tpu_custom_call" | custom-call | tf_op jit(solution)/shard_map/routed_backward/pallas_call | solution.py:571
  111.8 8.9 %emit.1 = (bf16[24,4096]{1,0:T(8,128)(2,1)}, f32[8,24]{1,0:T(8,128)}, bf16[1,4096,384]{2,1,0:T(8,128)(2,1)}, bf16[1,4096,384]{2,1,0:T(8,128)(2,1)}, bf16[1,384,4096]{2,1,0:T(8,128)(2,1)}) custom-call(bf16[24,4096]{1,0:T(8,128)(2,1)} %get-tuple-element.15.token, f32[8,24]{1,0:T(8,128)} %get-tuple-element.16.prob, ...), custom_call_target="tpu_custom_call" | custom-call | tf_op jit(solution)/shard_map/emit/pallas_call | solution.py:585

commit v3 on v2

--- a/solution.py
+++ b/solution.py
@@ -21,7 +21,7 @@
 BLOCK = 2 * TOK
 PLANE = 16 * BLOCK
 LINE = 4 * BLOCK
-STEP = 256
+STEP = 512
 X, Y, Z = 0, 1, 2
 ORDERS = ((Z, Y, X), (X, Z, Y), (Y, X, Z))
 T_AT, T_HALF = (0, 1536, 2816), (768, 640, 640)
@@ -58,7 +58,7 @@
     return tuple(out)
 
 
-def enter(co, core):
+def greet(co, core):
     barrier = pltpu.get_barrier_semaphore()
     for axis in (X, Y, Z):
         for by in (1, 2, 3):
@@ -66,7 +66,6 @@
                 barrier, inc=1, device_id=device(shifted(co, axis, by), core), device_id_type=MESH
             )
     pl.semaphore_signal(barrier, inc=1, device_id=device(co, 1 - core), device_id_type=MESH)
-    pl.semaphore_wait(barrier, 10)
 
 
 def remote(src, dst, send, recv, to):
@@ -118,13 +117,13 @@
 
 def kernel(
     tok, grd, routes_in, probs_in, perm_in, gate_w, up_w, down_w,
-    token_grad, prob_grad, gate_out, up_out, down_out,
+    token_grad, prob_grad, rows_out, delta_out, down_out,
     rows_t, rows_g, wgu, wd,
     gt0, gt1, gt2, gg0, gg1, gg2, st0, st1, st2, sg0, sg1, sg2, rt0, rt1, rt2, rg0, rg1, rg2,
     rr0, rr1, rr2, bs0, bs1, bs2, cs0, cs1, cs2,
     perm, delta, hid, gu,
     a1_s, a1_r, a2_s, a2_r, x_s, x_r, d_s, d_r, w_s, w_r, h_s, h_r,
-    y_s, y_r, b2_s, b2_r, b1_s, b1_r, l_s, o_s,
+    y_s, y_r, b2_s, b2_r, b1_s, b1_r, l_s, o_s, t_s,
 ):
     co, core = position()
     partner = device(co, 1 - core)
@@ -156,6 +155,7 @@
         outs.clear()
 
     H2 = 2 * HALF
+    greet(co, core)
     loads = [
         pltpu.make_async_copy(gate_w.at[0], wgu.at[:, 0:HALF], l_s.at[0]),
         pltpu.make_async_copy(up_w.at[0], wgu.at[:, HALF:H2], l_s.at[1]),
@@ -192,7 +192,7 @@
                 )
 
     pack(0, tok)
-    enter(co, core)
+    pl.semaphore_wait(pltpu.get_barrier_semaphore(), 10)
     first(0)
     pack(1, grd)
     first(1)
@@ -290,11 +290,17 @@
             out[0:CLASS, at + n * h:at + n * h + h] = full[:, 0:h]
             if q == 0 and p == 2 and n == 0:
                 pk[...] = full[:, h:h + 128]
+        cols = slice(at, at + 2 * h)
+        if q == 0:
+            c = pltpu.make_async_copy(rows_t.at[:, cols], rows_out.at[0:CLASS, cols], t_s.at[p])
+            c.start()
+            stores.append(c)
+        there = rows_out if q == 0 else rows_g
         send(
-            out.at[0:CLASS, at:at + 2 * h], out.at[CLASS:ROWS, at:at + 2 * h],
-            d_s.at[q, p], d_r.at[q, p], partner,
+            out.at[0:CLASS, cols], there.at[CLASS:ROWS, cols], d_s.at[q, p], d_r.at[q, p], partner
         )
 
+    stores = []
     second_own(0)
     second_pass(0)
     second_own(1)
@@ -338,11 +344,11 @@
         c.wait()
     for p in range(3):
         reorder(0, p, rows_t)
-    gu[:, 0:H2] = dot(rows_t[0:CLASS, :], wgu[:, 0:H2])
+    gu[:, 0:H2] = dot(rows_t[...], wgu[:, 0:H2])
     arrive(wgu.at[:, H2:H2 + HALF], w_s.at[0], w_r.at[0])
     arrive(wgu.at[:, H2 + HALF:2 * H2], w_s.at[1], w_r.at[1])
     arrive(wd.at[HALF:H2], w_s.at[2], w_r.at[2])
-    gu[:, H2:2 * H2] = dot(rows_t[0:CLASS, :], wgu[:, H2:2 * H2])
+    gu[:, H2:2 * H2] = dot(rows_t[...], wgu[:, H2:2 * H2])
     for p in range(3):
         reorder(1, p, rows_g)
 
@@ -352,22 +358,27 @@
     weight = jnp.sum(
         jnp.where(lane == 64 + expert_of(co), pk[...].astype(F32), 0.0), axis=1, keepdims=True
     )
-    prob = jnp.zeros((CLASS, 1), F32)
-    for n, (dl, hd) in enumerate(((delta, hid), (delta_o, hid_o))):
-        gate, up = gu[:, n * H2:n * H2 + HALF], gu[:, n * H2 + HALF:n * H2 + H2]
-        grad = dot(rows_g[0:CLASS, :], wd[n * HALF:n * HALF + HALF, :], ((1,), (1,)))
-        sig = jax.nn.sigmoid(gate)
-        active = gate * sig
-        hidden = active * up
-        scaled = weight * grad
-        dl[0:CLASS, 0:HALF] = (scaled * up * sig * (1.0 + gate * (1.0 - sig))).astype(BF)
-        dl[0:CLASS, HALF:H2] = (scaled * active).astype(BF)
-        hd[0:CLASS, :] = (weight * hidden).astype(BF)
-        prob = prob + jnp.sum(hidden * grad, axis=1, keepdims=True).astype(BF).astype(F32)
-    prob = jnp.where(lane == expert_of(co), prob, 0.0)
-    prob_hi = prob.astype(BF)
-    ptile[:, 0:128] = prob_hi
-    ptile[:, 128:256] = (prob - prob_hi.astype(F32)).astype(BF)
+    raws = [
+        dot(rows_g[0:CLASS, :], wd[n * HALF:n * HALF + HALF, :], ((1,), (1,))) for n in range(2)
+    ]
+    for r in range(0, CLASS, SLOTS):
+        rows = slice(r, r + SLOTS)
+        prob = jnp.zeros((SLOTS, 1), F32)
+        for n, (dl, hd) in enumerate(((delta, hid), (delta_o, hid_o))):
+            gate, up = gu[rows, n * H2:n * H2 + HALF], gu[rows, n * H2 + HALF:n * H2 + H2]
+            grad = raws[n][rows]
+            sig = jax.nn.sigmoid(gate)
+            active = gate * sig
+            hidden = active * up
+            scaled = weight[rows] * grad
+            dl[rows, 0:HALF] = (scaled * up * sig * (1.0 + gate * (1.0 - sig))).astype(BF)
+            dl[rows, HALF:H2] = (scaled * active).astype(BF)
+            hd[rows, :] = (weight[rows] * hidden).astype(BF)
+            prob = prob + jnp.sum(hidden * grad, axis=1, keepdims=True).astype(BF).astype(F32)
+        prob = jnp.where(lane[rows] == expert_of(co), prob, 0.0)
+        prob_hi = prob.astype(BF)
+        ptile[rows, 0:128] = prob_hi
+        ptile[rows, 128:256] = (prob - prob_hi.astype(F32)).astype(BF)
 
     def piece(p, c):
         h = CUT if c == 0 else T_HALF[p] - CUT
@@ -377,19 +388,20 @@
         a1, a2, a3 = ORDERS[p]
         at, h, cols = piece(p, c)
         if p == 0:
-            own, other = delta[0:CLASS, :], delta_o[...]
+            own, other = delta[...], delta_o[...]
         else:
             if c == 0:
-                rec[1][p][0:CLASS, :] = dot(perm[p - 1], delta[0:CLASS, :], ((0,), (0,))).astype(BF)
+                rec[1][p][0:CLASS, :] = dot(perm[p - 1], delta[...], ((0,), (0,))).astype(BF)
                 rec[1][p][CLASS:ROWS, :] = dot(perm[p - 1], delta_o[...], ((0,), (0,))).astype(BF)
             own, other = rec[1][p][0:CLASS, :], rec[1][p][CLASS:ROWS, :]
         if (p, c) == (2, 1):
             tiles = dot(perm[p - 1], ptile[...], ((0,), (0,))).astype(BF)
+        w = slice(at, at + 2 * h)
+        both = (
+            dot(own, wgu[w, 0:H2], ((1,), (1,))) + dot(other, wgu[w, H2:2 * H2], ((1,), (1,)))
+        ).astype(BF)
         for n in range(2):
-            w = slice(at + n * h, at + n * h + h)
-            val = (
-                dot(own, wgu[w, 0:H2], ((1,), (1,))) + dot(other, wgu[w, H2:2 * H2], ((1,), (1,)))
-            ).astype(BF)
+            val = both[:, n * h:n * h + h]
             if (p, c) == (2, 1):
                 val = jnp.concatenate([val, tiles[:, n * 128:n * 128 + 128]], axis=1)
             for b in range(4):
@@ -407,23 +419,16 @@
     for c in range(2):
         for p in range(3):
             input_part(p, c)
-    send(delta_o, delta.at[CLASS:ROWS], h_s.at[0], h_r.at[0], partner)
+    send(delta_o, delta_out.at[CLASS:ROWS], h_s.at[0], h_r.at[0], partner)
     send(hid_o, hid.at[CLASS:ROWS], h_s.at[1], h_r.at[1], partner)
+    c = pltpu.make_async_copy(delta, delta_out.at[0:CLASS], t_s.at[3])
+    c.start()
+    stores.append(c)
 
     stage_d = (rg0.at[0:CLASS, 0:STEP], rg0.at[CLASS:ROWS, 0:STEP])
-    stage_gu = (rg1, rg2)
 
     def down_out_copy(n, cols):
         return pltpu.make_async_copy(stage_d[n], down_out.at[0, :, cols], o_s.at[n])
-
-    def gate_up_copies(n, cols):
-        return [
-            pltpu.make_async_copy(
-                stage_gu[n].at[0:STEP, m * HALF:m * HALF + HALF], out.at[0, cols, :],
-                o_s.at[2 + 2 * n + m],
-            )
-            for m, out in enumerate((gate_out, up_out))
-        ]
 
     def down_step(i, carry):
         for n in range(2):
@@ -433,18 +438,6 @@
             cols = pl.ds(pl.multiple_of((2 * i + n) * STEP, STEP), STEP)
             stage_d[n][...] = dot(hid[...], rows_g[:, cols], ((0,), (0,))).astype(BF)
             down_out_copy(n, cols).start()
-        return carry
-
-    def gate_up_step(i, carry):
-        for n in range(2):
-            @pl.when(i > 0)
-            def _():
-                for c in gate_up_copies(n, slice(0, STEP)):
-                    c.wait()
-            cols = pl.ds(pl.multiple_of((2 * i + n) * STEP, STEP), STEP)
-            stage_gu[n][0:STEP, :] = dot(rows_t[:, cols], delta[...], ((0,), (0,))).astype(BF)
-            for c in gate_up_copies(n, cols):
-                c.start()
         return carry
 
     sums = gts
@@ -503,74 +496,71 @@
                 )
 
     relay(0)
-    for q, out in ((0, rows_t), (1, rows_g)):
-        for p in range(3):
-            at, h = at_of[q][p], half_of[q][p]
-            arrive(out.at[CLASS:ROWS, at:at + 2 * h], d_s.at[q, p], d_r.at[q, p])
-    arrive(delta.at[CLASS:ROWS], h_s.at[0], h_r.at[0])
+    for p in range(3):
+        cols = slice(G_AT[p], G_AT[p] + 2 * G_HALF[p])
+        arrive(rows_g.at[CLASS:ROWS, cols], d_s.at[1, p], d_r.at[1, p])
     arrive(hid.at[CLASS:ROWS], h_s.at[1], h_r.at[1])
-    lax.fori_loop(0, 8, down_step, 0)
+    lax.fori_loop(0, 2, down_step, 0)
     relay(1)
     line_sum(0)
-    lax.fori_loop(0, 6, gate_up_step, 0)
+    lax.fori_loop(2, 4, down_step, 0)
     line_sum(1)
-    lax.fori_loop(6, 8, gate_up_step, 0)
     finish(0)
     finish(1)
     for n in range(2):
         down_out_copy(n, slice(0, STEP)).wait()
-        for c in gate_up_copies(n, slice(0, STEP)):
-            c.wait()
+    for p in range(3):
+        cols = slice(T_AT[p], T_AT[p] + 2 * T_HALF[p])
+        arrive(rows_out.at[CLASS:ROWS, cols], d_s.at[0, p], d_r.at[0, p])
+    arrive(delta_out.at[CLASS:ROWS], h_s.at[0], h_r.at[0])
+    for c in stores:
+        c.wait()
     for c in weights:
         c.wait_send()
     settle()
 
 
-def emit_kernel(token, prob, gate, up, down, token_out, prob_out, gate_out, up_out, down_out, held, held_d, sems):
-    jobs = []
-    for n, (src, dst) in enumerate(((gate, gate_out), (up, up_out), (down, down_out))):
-        rows = src.shape[1] // 4
-        for i in range(4):
-            part = slice(i * rows, i * rows + rows)
-            mid = held_d.at[part] if n == 2 else held.at[n, part]
-            c = pltpu.make_async_copy(src.at[0, part], mid, sems.at[0, n, i])
-            c.start()
-            jobs.append((c, pltpu.make_async_copy(mid, dst.at[0, part], sems.at[1, n, i])))
-    token_out[...] = token[...]
-    prob_out[...] = prob[...]
-    for c, d in jobs:
-        c.wait()
-        d.start()
-    for c, d in jobs:
-        d.wait()
+def weight_kernel(token, prob, rows, delta, down, token_out, prob_out, gate_out, up_out, down_out):
+    grads = dot(rows[...], delta[...], ((0,), (0,))).astype(BF)
+    gate_out[0] = grads[:, 0:HALF]
+    up_out[0] = grads[:, HALF:2 * HALF]
+    down_out[...] = down[...]
+
+    @pl.when(pl.program_id(0) == 0)
+    def _():
+        token_out[...] = token[...]
+        prob_out[...] = prob[...]
 
 
 def on_device(tokens, out_grad, routes, gate_probs, gate_weight, up_weight, down_weight):
     vmem = pl.BlockSpec(memory_space=pltpu.VMEM)
     anywhere = pl.BlockSpec(memory_space=pl.ANY)
     dma = pltpu.SemaphoreType.DMA
-    shapes = [(ROWS, D), (ROWS, D), (D, 4 * HALF), (2 * HALF, D)]
+    shapes = [(CLASS, D), (ROWS, D), (D, 4 * HALF), (2 * HALF, D)]
     shapes += [(PLANE, 896), (PLANE, 768), (PLANE, 768)] + [(PLANE, 768)] * 3
     shapes += [(576, w) for w in T_SENT] + [(576, w) for w in G_HALF]
     shapes += [(ROWS, w) for w in T_SENT] + [(ROWS, w) for w in (640, 768, 768)]
     shapes += [(ROWS, w) for w in BACK]
     shapes += [(3, LINE, w) for w in BACK]
     shapes += [(3, BLOCK, w) for w in BACK]
-    shapes += [PERM.shape, (ROWS, 2 * HALF), (ROWS, HALF)]
+    shapes += [PERM.shape, (CLASS, 2 * HALF), (ROWS, HALF)]
     scratch = [pltpu.VMEM(s, BF) for s in shapes] + [pltpu.VMEM((CLASS, 4 * HALF), F32)]
     for s in ((2, 3, 3), (2, 3, 6), (2, 3, 3), (2, 3), (3,), (2,)) + ((2, 3, 3),) * 3:
         scratch += [dma(s), dma(s)]
-    scratch += [dma((4,)), dma((6,))]
-    shaped = (
-        jax.ShapeDtypeStruct((TOK, D), BF),
-        jax.ShapeDtypeStruct((TOP, TOK), F32),
-        jax.ShapeDtypeStruct((1, D, HALF), BF),
-        jax.ShapeDtypeStruct((1, D, HALF), BF),
-        jax.ShapeDtypeStruct((1, HALF, D), BF),
-    )
+    scratch += [dma((4,)), dma((2,)), dma((4,))]
+    token_shape = jax.ShapeDtypeStruct((TOK, D), BF)
+    prob_shape = jax.ShapeDtypeStruct((TOP, TOK), F32)
+    wide_shape = jax.ShapeDtypeStruct((1, D, HALF), BF)
+    down_shape = jax.ShapeDtypeStruct((1, HALF, D), BF)
     results = pl.pallas_call(
         kernel,
-        out_shape=shaped,
+        out_shape=(
+            token_shape,
+            prob_shape,
+            jax.ShapeDtypeStruct((ROWS, D), BF),
+            jax.ShapeDtypeStruct((ROWS, 2 * HALF), BF),
+            down_shape,
+        ),
         in_specs=[vmem] * 4 + [anywhere] * 4,
         out_specs=(vmem, vmem, anywhere, anywhere, anywhere),
         scratch_shapes=scratch,
@@ -582,14 +572,21 @@
         tokens, out_grad, routes.T, gate_probs.T, jnp.asarray(PERM, BF),
         gate_weight, up_weight, down_weight,
     )
+    whole = [pl.BlockSpec((TOK, D), lambda i: (0, 0)), pl.BlockSpec((TOP, TOK), lambda i: (0, 0))]
+    tall = pl.BlockSpec((1, STEP, HALF), lambda i: (0, i, 0))
+    flat = pl.BlockSpec((1, HALF, STEP), lambda i: (0, 0, i))
     token_grad, prob_grad, gate_grad, up_grad, down_grad = pl.pallas_call(
-        emit_kernel,
-        out_shape=shaped,
-        in_specs=[vmem] * 2 + [anywhere] * 3,
-        out_specs=(vmem, vmem, anywhere, anywhere, anywhere),
-        scratch_shapes=[pltpu.VMEM((2, D, HALF), BF), pltpu.VMEM((HALF, D), BF), dma((2, 3, 4))],
+        weight_kernel,
+        grid=(D // STEP,),
+        out_shape=(token_shape, prob_shape, wide_shape, wide_shape, down_shape),
+        in_specs=whole + [
+            pl.BlockSpec((ROWS, STEP), lambda i: (0, i)),
+            pl.BlockSpec((ROWS, 2 * HALF), lambda i: (0, 0)),
+            flat,
+        ],
+        out_specs=whole + [tall, tall, flat],
         compiler_params=pltpu.CompilerParams(vmem_limit_bytes=62 * 2**20),
-        name="emit",
+        name="weight_grads",
     )(*results)
     return token_grad, prob_grad.T, gate_grad, up_grad, down_grad
 

time: 121 us -> 117 us (0.967)
  Pallas kernels: 120 us -> 116 us
    pallas_call x2, Pallas kernels: 120 us -> 116 us  [the longest x1 104 us: on_device(): pl.pallas_call(kernel, out_shape=(token_shape, prob_shape, jax.ShapeDtype...]
where the time goes in v3:
time: 117 us
  Pallas kernels  116 us (99%)
    pallas_call x1, Pallas kernels, on_device(): pl.pallas_call(kernel, out_shape=(token_shape, prob_shape, jax.ShapeDtype...  104 us
    pallas_call x1, Pallas kernels, on_device(): pl.pallas_call(weight_kernel, grid=(D // STEP,), out_shape=(token_shape,...  12.4 us

profile of v3, /device:TPU:0, one launch (start us, length us, event | category | flops | bytes accessed | tf_op | source)
XLA Modules:
  0.0 116.9 jit_solution(12516862076518527549)
XLA Ops:
  0.6 103.8 %routed_backward.1 = (bf16[24,4096]{1,0:T(8,128)(2,1)}, f32[8,24]{1,0:T(8,128)}, bf16[768,4096]{1,0:T(8,128)(2,1)}, bf16[768,768]{1,0:T(8,128)(2,1)}, bf16[1,384,4096]{2,1,0:T(8,128)(2,1)}) custom-call(bf16[24,4096]{1,0:T(8,128)(2,1)} %tok.1, bf16[24,4096]{1,0:T(8,128)(2,1)} %grd.1, s32[8,24]{1,0:T(8,128)} %bitcast.3, bf16[8,24]{1,0:T(8,128)(2,1)} %bitcast.4, ...), custom_call_target="tpu_custom_call" | custom-call | tf_op jit(solution)/shard_map/routed_backward/pallas_call | solution.py:555
  104.5 12.4 %weight_grads.1 = (bf16[24,4096]{1,0:T(8,128)(2,1)}, f32[8,24]{1,0:T(8,128)}, bf16[1,4096,384]{2,1,0:T(8,128)(2,1)}, bf16[1,4096,384]{2,1,0:T(8,128)(2,1)}, bf16[1,384,4096]{2,1,0:T(8,128)(2,1)}) custom-call(bf16[24,4096]{1,0:T(8,128)(2,1)} %get-tuple-element.15.token, f32[8,24]{1,0:T(8,128)} %get-tuple-element.16.prob, ...), custom_call_target="tpu_custom_call" | custom-call | tf_op jit(solution)/shard_map/weight_grads/pallas_call | solution.py:578

commit v4 on v3

--- a/solution.py
+++ b/solution.py
@@ -22,6 +22,7 @@
 PLANE = 16 * BLOCK
 LINE = 4 * BLOCK
 STEP = 512
+TALL = 1024
 X, Y, Z = 0, 1, 2
 ORDERS = ((Z, Y, X), (X, Z, Y), (Y, X, Z))
 T_AT, T_HALF = (0, 1536, 2816), (768, 640, 640)
@@ -520,16 +521,41 @@
     settle()
 
 
-def weight_kernel(token, prob, rows, delta, down, token_out, prob_out, gate_out, up_out, down_out):
+def weight_kernel(
+    token, prob, rows, delta, down, token_out, prob_out, gate_out, up_out, down_out, held, i_s, o_s
+):
+    step = pl.program_id(0)
+    quarters = [slice(n * SLOTS, n * SLOTS + SLOTS) for n in range(4)]
+    ins = [
+        pltpu.make_async_copy(down.at[0, part], held.at[part], i_s.at[n])
+        for n, part in enumerate(quarters)
+    ]
+    outs = [
+        pltpu.make_async_copy(held.at[part], down_out.at[0, part], o_s.at[n])
+        for n, part in enumerate(quarters)
+    ]
+
+    @pl.when(step == 0)
+    def _():
+        for c in ins:
+            c.start()
+        token_out[...] = token[...]
+        prob_out[...] = prob[...]
+
     grads = dot(rows[...], delta[...], ((0,), (0,))).astype(BF)
     gate_out[0] = grads[:, 0:HALF]
     up_out[0] = grads[:, HALF:2 * HALF]
-    down_out[...] = down[...]
-
-    @pl.when(pl.program_id(0) == 0)
+
+    @pl.when(step == 1)
     def _():
-        token_out[...] = token[...]
-        prob_out[...] = prob[...]
+        for c, d in zip(ins, outs):
+            c.wait()
+            d.start()
+
+    @pl.when(step == D // TALL - 1)
+    def _():
+        for d in outs:
+            d.wait()
 
 
 def on_device(tokens, out_grad, routes, gate_probs, gate_weight, up_weight, down_weight):
@@ -573,18 +599,18 @@
         gate_weight, up_weight, down_weight,
     )
     whole = [pl.BlockSpec((TOK, D), lambda i: (0, 0)), pl.BlockSpec((TOP, TOK), lambda i: (0, 0))]
-    tall = pl.BlockSpec((1, STEP, HALF), lambda i: (0, i, 0))
-    flat = pl.BlockSpec((1, HALF, STEP), lambda i: (0, 0, i))
+    tall = pl.BlockSpec((1, TALL, HALF), lambda i: (0, i, 0))
     token_grad, prob_grad, gate_grad, up_grad, down_grad = pl.pallas_call(
         weight_kernel,
-        grid=(D // STEP,),
+        grid=(D // TALL,),
         out_shape=(token_shape, prob_shape, wide_shape, wide_shape, down_shape),
         in_specs=whole + [
-            pl.BlockSpec((ROWS, STEP), lambda i: (0, i)),
+            pl.BlockSpec((ROWS, TALL), lambda i: (0, i)),
             pl.BlockSpec((ROWS, 2 * HALF), lambda i: (0, 0)),
-            flat,
+            anywhere,
         ],
-        out_specs=whole + [tall, tall, flat],
+        out_specs=whole + [tall, tall, anywhere],
+        scratch_shapes=[pltpu.VMEM((HALF, D), BF), dma((4,)), dma((4,))],
         compiler_params=pltpu.CompilerParams(vmem_limit_bytes=62 * 2**20),
         name="weight_grads",
     )(*results)

time: 117 us -> 115 us (0.983)
  Pallas kernels: 116 us -> 114 us
    pallas_call x1, Pallas kernels: 12.4 us -> 10.4 us  [on_device(): pl.pallas_call(weight_kernel, grid=(D // TALL,), out_shape=(token_shape,...]
where the time goes in v4:
time: 115 us
  Pallas kernels  114 us (99%)
    pallas_call x1, Pallas kernels, on_device(): pl.pallas_call(kernel, out_shape=(token_shape, prob_shape, jax.ShapeDtype...  104 us
    pallas_call x1, Pallas kernels, on_device(): pl.pallas_call(weight_kernel, grid=(D // TALL,), out_shape=(token_shape,...  10.4 us

profile of v4, /device:TPU:0, one launch (start us, length us, event | category | flops | bytes accessed | tf_op | source)
XLA Modules:
  0.0 115.0 jit_solution(14499742885496336176)
XLA Ops:
  0.6 103.8 %routed_backward.1 = (bf16[24,4096]{1,0:T(8,128)(2,1)}, f32[8,24]{1,0:T(8,128)}, bf16[768,4096]{1,0:T(8,128)(2,1)}, bf16[768,768]{1,0:T(8,128)(2,1)}, bf16[1,384,4096]{2,1,0:T(8,128)(2,1)}) custom-call(bf16[24,4096]{1,0:T(8,128)(2,1)} %tok.1, bf16[24,4096]{1,0:T(8,128)(2,1)} %grd.1, s32[8,24]{1,0:T(8,128)} %bitcast.3, bf16[8,24]{1,0:T(8,128)(2,1)} %bitcast.4, ...), custom_call_target="tpu_custom_call" | custom-call | tf_op jit(solution)/shard_map/routed_backward/pallas_call | solution.py:581
  104.5 10.4 %weight_grads.1 = (bf16[24,4096]{1,0:T(8,128)(2,1)}, f32[8,24]{1,0:T(8,128)}, bf16[1,4096,384]{2,1,0:T(8,128)(2,1)}, bf16[1,4096,384]{2,1,0:T(8,128)(2,1)}, bf16[1,384,4096]{2,1,0:T(8,128)(2,1)}) custom-call(bf16[24,4096]{1,0:T(8,128)(2,1)} %get-tuple-element.15.token, f32[8,24]{1,0:T(8,128)} %get-tuple-element.16.prob, ...), custom_call_target="tpu_custom_call" | custom-call | tf_op jit(solution)/shard_map/weight_grads/pallas_call | solution.py:603
